TPU v7x, 32 devices: a whole 2x2x4 slice. The times are simulated.
32 devices in a mesh: rep: 4 (over x, core), shard: 8 (over z, y).
Axes of the slice: x: 2, y: 2, z: 4, core: 2. Of those that a mesh axis runs over, the one named last changes fastest.
Arguments:
- inputs: bfloat16 [4, 2048, 1088], P('rep', 'shard'), may hold values from -6 to 6
- w_attn: bfloat16 [2, 1088, 3264], P(None, 'shard'), may hold values from -0.1875 to 0.1875
- w_out: bfloat16 [2, 1088, 1088], P(None, 'shard'), may hold values from -2 to 2
- w_fc: bfloat16 [2, 1088, 4352], P(None, 'shard'), may hold values from -0.1875 to 0.1875
- w_proj: bfloat16 [2, 4352, 1088], P(None, 'shard'), may hold values from -0.09375 to 0.09375
- norm_gains: float32 [2, 2, 1088], P(None, None, 'shard'), may hold values from 0.25 to 1.75
- norm_biases: float32 [2, 2, 1088], P(None, None, 'shard'), may hold values from -1.5 to 1.5
- dense_biases: float32 [2, 4, 1088], P(None, None, 'shard'), may hold values from -1.5 to 1.5
- fc_bias: float32 [2, 4352], P(None, 'shard'), may hold values from -2.5 to 2.5
- cotangent: bfloat16 [4, 2048, 1088], P('rep', 'shard'), may hold values from -6 to 6
Outputs:
- result: bfloat16 [4, 2048, 1088], P('rep', 'shard')
- input_grad: float32 [4, 2048, 1088], P('rep', 'shard')
- grad_w_attn: float32 [2, 1088, 3264], P(None, 'shard')
- grad_w_out: float32 [2, 1088, 1088], P(None, 'shard')
- grad_w_fc: float32 [2, 1088, 4352], P(None, 'shard')
- grad_w_proj: float32 [2, 4352, 1088], P(None, 'shard')
- grad_norm_gains: float32 [2, 2, 1088], P(None, None, 'shard')
- grad_norm_biases: float32 [2, 2, 1088], P(None, None, 'shard')
- grad_dense_biases: float32 [2, 4, 1088], P(None, None, 'shard')
- grad_fc_bias: float32 [2, 4352], P(None, 'shard')
All inputs are finite; a program needn't handle non-finite values.
Results may differ from a plain program's by a relative error of at most 0.023.
Values may be sent and summed in bfloat16 or wider, within the bound.
A program may use at most 384 MiB of HBM per device.

v0:
```python
import jax
import jax.numpy as jnp
from jax import lax
from jax.sharding import PartitionSpec as P

HEADS = 17
HEAD_SIZE = 64
LAYERS = 2


eps = 1e-05
masked = -1e30


def passed_along(block, axis, distance):
    devices = range(lax.axis_size(axis))
    route = [((i - distance) % len(devices), i) for i in devices]
    return lax.ppermute(block, axis, route)


def norm_forward(x, gain, bias):
    centre = jnp.mean(x, axis=-1, keepdims=True)
    centred = x - centre
    rstd = lax.rsqrt(jnp.mean(centred * centred, axis=-1, keepdims=True) + eps)
    normal = centred * rstd
    return (normal * gain + bias, (normal, rstd))


def norm_backward(grad, saved, gain):
    normal, rstd = saved
    scaled = grad * gain
    gain_grad = jnp.sum(grad * normal, axis=0)
    bias_grad = jnp.sum(grad, axis=0)
    inner = scaled - jnp.mean(scaled, axis=-1, keepdims=True)
    inner = inner - normal * jnp.mean(scaled * normal, axis=-1, keepdims=True)
    return (rstd * inner, gain_grad, bias_grad)


def forward_rows(acts, weight):
    return jnp.dot(
        acts,
        lax.all_gather(weight, "shard", axis=0, tiled=True),
        preferred_element_type=jnp.float32,
    )


def backward_rows(grad, weight):
    return lax.dot_general(
        grad,
        lax.all_gather(weight, "shard", axis=0, tiled=True),
        (((1,), (1,)), ((), ())),
        preferred_element_type=jnp.float32,
    )


def weight_grad(acts, grad):
    return lax.psum_scatter(
        lax.dot_general(
            acts, grad, (((0,), (0,)), ((), ())), preferred_element_type=jnp.float32
        ).astype(jnp.bfloat16),
        "shard",
        scatter_dimension=0,
        tiled=True,
    ).astype(jnp.float32)


def attend_forward(query, keys, values, query_pos):
    seqs, span, heads, size = query.shape
    scale = HEAD_SIZE ** (-0.5)
    pieces = (
        lax.all_gather(keys, "shard", axis=1, tiled=True),
        lax.all_gather(values, "shard", axis=1, tiled=True),
    )
    running = jnp.full((seqs, span, heads), masked, jnp.float32)
    count = pieces[0].shape[1]
    key_piece = pieces[0].reshape(seqs, count, heads, size)
    value_piece = pieces[1].reshape(seqs, count, heads, size)
    scores = (
        jnp.einsum("sqhd,skhd->sqhk", query, key_piece, preferred_element_type=jnp.float32) * scale
    )
    key_pos = jnp.arange(count, dtype=jnp.int32)
    allowed = (key_pos[None, :] <= query_pos[:, None])[None, :, None, :]
    scores = jnp.where(allowed, scores, masked)
    newest = jnp.maximum(running, jnp.max(scores, axis=-1))
    probs = jnp.where(allowed, jnp.exp(scores - newest[..., None]), 0.0)
    mixed = jnp.einsum(
        "sqhk,skhd->sqhd",
        probs.astype(jnp.bfloat16),
        value_piece,
        preferred_element_type=jnp.float32,
    )
    total = jnp.sum(probs, axis=-1)
    return (mixed / total[..., None], newest + jnp.log(total), None)


def attend_backward(query, keys, values, grad_out, logsum, delta, query_pos):
    seqs, span, heads, size = query.shape
    scale = HEAD_SIZE ** (-0.5)
    count = lax.axis_size("shard")
    index = lax.axis_index("shard")
    zeros_kv = jnp.zeros(keys.shape, jnp.float32)
    state = (keys, values, zeros_kv, zeros_kv, jnp.zeros(query.shape, jnp.float32))

    def one_piece(state, turn):
        key_blk, value_blk, key_grad, value_grad, query_grad = state
        source = (index + turn) % count
        start = source * span
        key_piece = key_blk.reshape(seqs, span, heads, size)
        value_piece = value_blk.reshape(seqs, span, heads, size)
        scores = (
            jnp.einsum("sqhd,skhd->sqhk", query, key_piece, preferred_element_type=jnp.float32)
            * scale
        )
        key_pos = start + jnp.arange(span, dtype=jnp.int32)
        allowed = (key_pos[None, :] <= query_pos[:, None])[None, :, None, :]
        probs = jnp.where(allowed, jnp.exp(scores - logsum[..., None]), 0.0)
        prob_grad = jnp.einsum(
            "sqhd,skhd->sqhk", grad_out, value_piece, preferred_element_type=jnp.float32
        )
        score_grad = (probs * (prob_grad - delta[..., None]) * scale).astype(jnp.bfloat16)
        query_grad = query_grad + jnp.einsum(
            "sqhk,skhd->sqhd", score_grad, key_piece, preferred_element_type=jnp.float32
        )
        key_add = jnp.einsum(
            "sqhk,sqhd->skhd", score_grad, query, preferred_element_type=jnp.float32
        )
        value_add = jnp.einsum(
            "sqhk,sqhd->skhd",
            probs.astype(jnp.bfloat16),
            grad_out,
            preferred_element_type=jnp.float32,
        )
        key_grad = key_grad + key_add.reshape(key_grad.shape)
        value_grad = value_grad + value_add.reshape(value_grad.shape)
        key_blk, value_blk = passed_along((key_blk, value_blk), "shard", -1)
        key_grad, value_grad = (
            passed_along(key_grad.astype(jnp.bfloat16), "shard", -1).astype(key_grad.dtype),
            passed_along(value_grad.astype(jnp.bfloat16), "shard", -1).astype(value_grad.dtype),
        )
        return (key_blk, value_blk, key_grad, value_grad, query_grad)

    def two_pieces(turn, state):
        state = one_piece(state, 2 * turn)
        return one_piece(state, 2 * turn + 1)

    state = lax.fori_loop(0, count // 2, two_pieces, state)
    return (state[4], state[2], state[3])


def layer_forward(
    x, w_attn, w_out, w_fc, w_proj, gains, shifts, dense, fc_shift, query_pos, seqs, span
):
    width = x.shape[1]
    normed, saved_one = norm_forward(x, gains[0], shifts[0])
    normed_low = normed.astype(jnp.bfloat16)
    mixed = forward_rows(normed_low, w_attn)
    query = (mixed[:, :width] + dense[0]).astype(jnp.bfloat16).reshape(seqs, span, HEADS, HEAD_SIZE)
    keys = mixed[:, width : 2 * width].astype(jnp.bfloat16).reshape(seqs, span, width)
    values = (mixed[:, 2 * width :] + dense[1]).astype(jnp.bfloat16).reshape(seqs, span, width)
    attended, logsum, gathered = attend_forward(query, keys, values, query_pos)
    attended_low = attended.reshape(seqs * span, width).astype(jnp.bfloat16)
    middle = x + forward_rows(attended_low, w_out) + dense[2]
    normed2, saved_two = norm_forward(middle, gains[1], shifts[1])
    normed2_low = normed2.astype(jnp.bfloat16)
    hidden = forward_rows(normed2_low, w_fc) + fc_shift
    active_low = jax.nn.gelu(hidden, approximate=True).astype(jnp.bfloat16)
    output = middle + forward_rows(active_low, w_proj) + dense[3]
    kept = (
        saved_one,
        normed_low,
        query,
        keys,
        values,
        attended,
        logsum,
        attended_low,
        saved_two,
        normed2_low,
        hidden,
        active_low,
        gathered,
    )
    return (output, kept)


def layer_backward(grad, kept, w_attn, w_out, w_fc, w_proj, gains, query_pos, seqs, span):
    (
        saved_one,
        normed_low,
        query,
        keys,
        values,
        attended,
        logsum,
        attended_low,
        saved_two,
        normed2_low,
        hidden,
        active_low,
        gathered,
    ) = kept
    width = grad.shape[1]
    proj_bias_grad = jnp.sum(grad, axis=0)
    grad_low = grad.astype(jnp.bfloat16)
    active_grad = backward_rows(grad_low, w_proj)
    proj_grad = weight_grad(active_low, grad_low)
    gelu_pull = jax.vjp(lambda value: jax.nn.gelu(value, approximate=True), hidden)[1]
    hidden_grad = gelu_pull(active_grad)[0]
    fc_bias_grad = jnp.sum(hidden_grad, axis=0)
    hidden_low = hidden_grad.astype(jnp.bfloat16)
    normed2_grad = backward_rows(hidden_low, w_fc)
    fc_grad = weight_grad(normed2_low, hidden_low)
    middle_norm, gain_two, shift_two = norm_backward(normed2_grad, saved_two, gains[1])
    middle_grad = grad + middle_norm
    out_bias_grad = jnp.sum(middle_grad, axis=0)
    middle_low = middle_grad.astype(jnp.bfloat16)
    attended_grad = backward_rows(middle_low, w_out).astype(jnp.bfloat16)
    out_grad = weight_grad(attended_low, middle_low)
    grad_heads = attended_grad.reshape(seqs, span, HEADS, HEAD_SIZE)
    delta = jnp.sum(grad_heads.astype(jnp.float32) * attended, axis=-1)
    query_grad, key_grad, value_grad = attend_backward(
        query, keys, values, grad_heads, logsum, delta, query_pos
    )
    query_grad = query_grad.reshape(seqs * span, width)
    key_grad = key_grad.reshape(seqs * span, width)
    value_grad = value_grad.reshape(seqs * span, width)
    query_bias_grad = jnp.sum(query_grad, axis=0)
    value_bias_grad = jnp.sum(value_grad, axis=0)
    mixed_low = jnp.concatenate([query_grad, key_grad, value_grad], axis=1).astype(jnp.bfloat16)
    normed_grad = backward_rows(mixed_low, w_attn)
    attn_grad = weight_grad(normed_low, mixed_low)
    input_norm, gain_one, shift_one = norm_backward(normed_grad, saved_one, gains[0])
    input_grad = middle_grad + input_norm
    small = (
        lax.psum_scatter(
            jnp.stack([gain_one, gain_two]).astype(jnp.bfloat16),
            "shard",
            scatter_dimension=1,
            tiled=True,
        ).astype(jnp.float32),
        lax.psum_scatter(
            jnp.stack([shift_one, shift_two]).astype(jnp.bfloat16),
            "shard",
            scatter_dimension=1,
            tiled=True,
        ).astype(jnp.float32),
        lax.psum_scatter(
            jnp.stack([query_bias_grad, value_bias_grad, out_bias_grad, proj_bias_grad]).astype(
                jnp.bfloat16
            ),
            "shard",
            scatter_dimension=1,
            tiled=True,
        ).astype(jnp.float32),
        lax.psum_scatter(
            fc_bias_grad.astype(jnp.bfloat16), "shard", scatter_dimension=0, tiled=True
        ).astype(jnp.float32),
    )
    return (
        input_grad,
        (attn_grad, out_grad, fc_grad, proj_grad, small[0], small[1], small[2], small[3]),
    )


def body(
    inputs, w_attn, w_out, w_fc, w_proj, norm_gains, norm_biases, dense_biases, fc_bias, cotangent
):
    seqs, span, width = inputs.shape
    index = lax.axis_index("shard")
    query_pos = index * span + jnp.arange(span, dtype=jnp.int32)
    gains_all, shifts_all, dense_all, fc_all = (
        lax.all_gather(norm_gains, "shard", axis=2, tiled=True),
        lax.all_gather(norm_biases, "shard", axis=2, tiled=True),
        lax.all_gather(dense_biases, "shard", axis=2, tiled=True),
        lax.all_gather(fc_bias, "shard", axis=1, tiled=True),
    )
    state = inputs.reshape(seqs * span, width).astype(jnp.float32)
    stored = []
    for layer in range(LAYERS):
        state, kept = layer_forward(
            state,
            w_attn[layer],
            w_out[layer],
            w_fc[layer],
            w_proj[layer],
            gains_all[layer],
            shifts_all[layer],
            dense_all[layer],
            fc_all[layer],
            query_pos,
            seqs,
            span,
        )
        stored.append(kept)
    result = state.reshape(seqs, span, width).astype(jnp.bfloat16)
    grad = cotangent.reshape(seqs * span, width).astype(jnp.float32)
    collected = [None] * LAYERS
    for layer in reversed(range(LAYERS)):
        grad, parts = layer_backward(
            grad,
            stored[layer],
            w_attn[layer],
            w_out[layer],
            w_fc[layer],
            w_proj[layer],
            gains_all[layer],
            query_pos,
            seqs,
            span,
        )
        sliced = (
            lax.psum_scatter(
                parts[0].astype(jnp.bfloat16), "rep", scatter_dimension=1, tiled=True
            ).astype(jnp.float32),
            lax.psum_scatter(
                parts[1].astype(jnp.bfloat16), "rep", scatter_dimension=1, tiled=True
            ).astype(jnp.float32),
            lax.psum_scatter(
                parts[2].astype(jnp.bfloat16), "rep", scatter_dimension=1, tiled=True
            ).astype(jnp.float32),
            lax.psum_scatter(
                parts[3].astype(jnp.bfloat16), "rep", scatter_dimension=1, tiled=True
            ).astype(jnp.float32),
        )
        large = (
            lax.all_gather(sliced[0].astype(jnp.bfloat16), "rep", axis=1, tiled=True).astype(
                jnp.float32
            ),
            lax.all_gather(sliced[1].astype(jnp.bfloat16), "rep", axis=1, tiled=True).astype(
                jnp.float32
            ),
            lax.all_gather(sliced[2].astype(jnp.bfloat16), "rep", axis=1, tiled=True).astype(
                jnp.float32
            ),
            lax.all_gather(sliced[3].astype(jnp.bfloat16), "rep", axis=1, tiled=True).astype(
                jnp.float32
            ),
        )
        little = lax.psum((parts[4], parts[5], parts[6], parts[7]), "rep")
        parts = (large[0], large[1], large[2], large[3], little[0], little[1], little[2], little[3])
        collected[layer] = parts
    stacked = [jnp.stack([collected[layer][item] for layer in range(LAYERS)]) for item in range(8)]
    input_grad = grad.reshape(seqs, span, width)
    return (
        result,
        input_grad,
        stacked[0],
        stacked[1],
        stacked[2],
        stacked[3],
        stacked[4],
        stacked[5],
        stacked[6],
        stacked[7],
    )


def solution(mesh):
    in_specs = (
        P("rep", "shard", None),
        P(None, "shard", None),
        P(None, "shard", None),
        P(None, "shard", None),
        P(None, "shard", None),
        P(None, None, "shard"),
        P(None, None, "shard"),
        P(None, None, "shard"),
        P(None, "shard"),
        P("rep", "shard", None),
    )
    out_specs = (
        P("rep", "shard", None),
        P("rep", "shard", None),
        P(None, "shard", None),
        P(None, "shard", None),
        P(None, "shard", None),
        P(None, "shard", None),
        P(None, None, "shard"),
        P(None, None, "shard"),
        P(None, None, "shard"),
        P(None, "shard"),
    )
    return jax.shard_map(body, mesh=mesh, in_specs=in_specs, out_specs=out_specs, check_vma=False)
```

profile of v0, /device:TPU:0, one launch (start us, length us, event | category | flops | bytes accessed | tf_op | source)
XLA Modules:
  0.0 3521.6 jit_solution(4280254685904961128)
XLA Ops:
  10.5 39.1 %all_gather.80 = f32[2,2,1088]{1,0,2:T(2,128)S(1)} all-gather(f32[2,2,136]{1,0,2:T(2,128)S(1)} %copy.94), channel_id=1, replica_groups=mesh['rep'=4,'shard'=8] {'shard'}, dimensions={2}, use_global_device_ids=true | all-gather | bytes 19584 | tf_op jit(solution)/shard_map/all_gather | solution.py:272
  49.5 36.0 %all_gather.81 = f32[2,2,1088]{1,0,2:T(2,128)S(1)} all-gather(f32[2,2,136]{1,0,2:T(2,128)S(1)} %copy.95), channel_id=1, replica_groups=mesh['rep'=4,'shard'=8] {'shard'}, dimensions={2}, use_global_device_ids=true | all-gather | bytes 19584 | tf_op jit(solution)/shard_map/all_gather | solution.py:273
  151.0 35.2 %all_gather.83 = f32[2,4,1088]{1,0,2:T(2,128)S(1)} all-gather(f32[2,4,136]{1,0,2:T(2,128)S(1)} %copy.96), channel_id=1, replica_groups=mesh['rep'=4,'shard'=8] {'shard'}, dimensions={2}, use_global_device_ids=true | all-gather | bytes 39168 | tf_op jit(solution)/shard_map/all_gather | solution.py:274
  225.0 30.9 all-gather.12
  337.9 35.3 %all-gather.46.cloned.1.call-done = bf16[1,1088,1088]{2,1,0:T(8,128)(2,1)} async-done(((bf16[1,136,1088]{2,1,0:T(8,128)(2,1)}), bf16[1,1088,1088]{2,1,0:T(8,128)(2,1)}) %all-gather.46.cloned.1.call-update) | async-done | bytes 2367504 | tf_op jit(solution)/shard_map/all_gather | solution.py:42
  376.4 136.5 %all-gather.48.cloned.1.call-done = bf16[1,1088,4352]{2,1,0:T(8,128)(2,1)} async-done(((bf16[1,136,4352]{2,1,0:T(8,128)(2,1)}), bf16[1,1088,4352]{2,1,0:T(8,128)(2,1)}) %all-gather.48.cloned.1.call-update) | async-done | bytes 9469968 | tf_op jit(solution)/shard_map/all_gather | solution.py:42
  522.0 137.0 %all-gather.50.cloned.1.call-done = bf16[1,4352,1088]{2,1,0:T(8,128)(2,1)} async-done(((bf16[1,544,1088]{2,1,0:T(8,128)(2,1)}), bf16[1,4352,1088]{2,1,0:T(8,128)(2,1)}) %all-gather.50.cloned.1.call-update) | async-done | bytes 9469968 | tf_op jit(solution)/shard_map/all_gather | solution.py:42
  668.6 101.5 %all-gather.52.cloned.1.call-done = bf16[1,1088,3264]{2,1,0:T(8,128)(2,1)} async-done(((bf16[1,136,3264]{2,1,0:T(8,128)(2,1)}), bf16[1,1088,3264]{2,1,0:T(8,128)(2,1)}) %all-gather.52.cloned.1.call-update) | async-done | bytes 7102480 | tf_op jit(solution)/shard_map/all_gather | solution.py:42
  786.7 69.4 %all-gather.56.cloned.1.call-done = bf16[2048,1088]{0,1:T(8,128)(2,1)} async-done(((bf16[256,1088]{0,1:T(8,128)(2,1)}), bf16[2048,1088]{0,1:T(8,128)(2,1)}) %all-gather.56.cloned.1.call-update) | async-done | bytes 4456464 | tf_op jit(solution)/shard_map/all_gather | solution.py:71
  888.5 45.8 %all-gather.54.cloned.1.call-done = bf16[2048,1088]{0,1:T(8,128)(2,1)} async-done(((bf16[256,1088]{0,1:T(8,128)(2,1)}), bf16[2048,1088]{0,1:T(8,128)(2,1)}) %all-gather.54.cloned.1.call-update) | async-done | bytes 4456464 | tf_op jit(solution)/shard_map/all_gather | solution.py:72
  953.2 35.0 all-gather.58.cloned.1.call-done
  991.6 135.8 %all-gather.60.cloned.1.call-done = bf16[1,1088,4352]{2,1,0:T(8,128)(2,1)} async-done(((bf16[1,136,4352]{2,1,0:T(8,128)(2,1)}), bf16[1,1088,4352]{2,1,0:T(8,128)(2,1)}) %all-gather.60.cloned.1.call-update) | async-done | bytes 9469968 | tf_op jit(solution)/shard_map/all_gather | solution.py:42
  1136.5 136.9 %all-gather.62.cloned.1.call-done = bf16[1,4352,1088]{2,1,0:T(8,128)(2,1)} async-done(((bf16[1,544,1088]{2,1,0:T(8,128)(2,1)}), bf16[1,4352,1088]{2,1,0:T(8,128)(2,1)}) %all-gather.62.cloned.1.call-update) | async-done | bytes 9469968 | tf_op jit(solution)/shard_map/all_gather | solution.py:42
  1288.5 399.2 %while.48 = (s32[]{:T(128)}, bf16[1,256,1088]{1,2,0:T(8,128)(2,1)}, bf16[1,256,1088]{1,2,0:T(8,128)(2,1)}, f32[1,256,1088]{1,2,0:T(8,128)}, f32[1,256,1088]{1,2,...) while((s32[]{:T(128)}, bf16[1,256,1088]{1,2,0:T(8,128)(2,1)}, ...), condition=%wide.region_16.17_spmd.clone, body=%wide.region_15.16_spmd.clone.sunk | while | flops 1455440640 | bytes 107459488 | solution.py:146
  1766.0 440.7 %while.49 = (s32[]{:T(128)}, bf16[1,256,1088]{1,2,0:T(8,128)(2,1)}, bf16[1,256,1088]{1,2,0:T(8,128)(2,1)}, f32[1,256,1088]{1,2,0:T(8,128)}, f32[1,256,1088]{1,2,...) while((s32[]{:T(128)}, bf16[1,256,1088]{1,2,0:T(8,128)(2,1)}, ...), condition=%wide.region_23.24_spmd.clone, body=%wide.region_22.23_spmd.clone.sunk | while | flops 1455440640 | bytes 107459488 | solution.py:146
  2223.7 38.7 %reduce-scatter.51.cloned.1.call-done = bf16[544,1088]{1,0:T(8,128)(2,1)} async-done(((bf16[4352,1088]{1,0:T(8,128)(2,1)}), bf16[544,1088]{1,0:T(8,128)(2,1)}) %reduce-scatter.51.cloned.1.call-update) | async-done | bytes 1183760 | tf_op jit(solution)/shard_map/reduce_scatter | solution.py:57
  2265.0 172.2 %reduce-scatter.53.cloned.1.call-done = bf16[544,1088]{1,0:T(8,128)(2,1)} async-done(((bf16[4352,1088]{1,0:T(8,128)(2,1)}), bf16[544,1088]{1,0:T(8,128)(2,1)}) %reduce-scatter.53.cloned.1.call-update) | async-done | bytes 1183760 | tf_op jit(solution)/shard_map/reduce_scatter | solution.py:57
  2439.8 164.2 %reduce-scatter.47.cloned.1.call-done = bf16[136,4352]{1,0:T(8,128)(2,1)} async-done(((bf16[1088,4352]{1,0:T(8,128)(2,1)}), bf16[136,4352]{1,0:T(8,128)(2,1)}) %reduce-scatter.47.cloned.1.call-update) | async-done | bytes 1183760 | tf_op jit(solution)/shard_map/reduce_scatter | solution.py:57
  2607.7 69.5 %reduce-scatter.71.cloned.1.call-done = bf16[136,1088]{1,0:T(8,128)(2,1)} async-done(((bf16[1088,1088]{1,0:T(8,128)(2,1)}), bf16[136,1088]{1,0:T(8,128)(2,1)}) %reduce-scatter.71.cloned.1.call-update) | async-done | bytes 295952
  2679.3 71.8 %reduce-scatter.73.cloned.1.call-done = bf16[136,1088]{1,0:T(8,128)(2,1)} async-done(((bf16[1088,1088]{1,0:T(8,128)(2,1)}), bf16[136,1088]{1,0:T(8,128)(2,1)}) %reduce-scatter.73.cloned.1.call-update) | async-done | bytes 295952
  2753.2 164.7 %reduce-scatter.49.cloned.1.call-done = bf16[136,4352]{1,0:T(8,128)(2,1)} async-done(((bf16[1088,4352]{1,0:T(8,128)(2,1)}), bf16[136,4352]{1,0:T(8,128)(2,1)}) %reduce-scatter.49.cloned.1.call-update) | async-done | bytes 1183760 | tf_op jit(solution)/shard_map/reduce_scatter | solution.py:57
  2921.6 130.6 %reduce-scatter.43.cloned.1.call-done = bf16[136,3264]{1,0:T(8,128)(2,1)} async-done(((bf16[1088,3264]{1,0:T(8,128)(2,1)}), bf16[136,3264]{1,0:T(8,128)(2,1)}) %reduce-scatter.43.cloned.1.call-update) | async-done | bytes 887824 | tf_op jit(solution)/shard_map/reduce_scatter | solution.py:57
  3054.9 131.5 %reduce-scatter.45.cloned.1.call-done = bf16[136,3264]{1,0:T(8,128)(2,1)} async-done(((bf16[1088,3264]{1,0:T(8,128)(2,1)}), bf16[136,3264]{1,0:T(8,128)(2,1)}) %reduce-scatter.45.cloned.1.call-update) | async-done | bytes 887824 | tf_op jit(solution)/shard_map/reduce_scatter | solution.py:57
  3222.0 37.6 %all-reduce.11 = (bf16[2,1088]{1,0:T(2,128)(2,1)S(1)}, bf16[2,1088]{1,0:T(2,128)(2,1)S(1)}, bf16[2,1088]{1,0:T(2,128)(2,1)S(1)}, bf16[2,1088]{1,0:T(2,128)(2,1)S...) all-reduce(bf16[2,1088]{1,0:T(2,128)(2,1)S(1)} %pad_maximum_fusion., ...), channel_id=31, replica_groups=mesh['rep'=4,'shard'=8] {'shard'}, use_global_device_ids=true, to_apply=%region_48.49.clone | all-reduce | flops 26112 | bytes 104448
  (830 shorter events, 1547.9 us)
Async XLA Ops:
  217.1 295.8 %all-gather.48.cloned.1.call-start = ((), (), s32[]{:S(2)}) async-start(), calls=%async_computation.28 | async-start | bytes 10653696 | tf_op jit(solution)/shard_map/all_gather | solution.py:42
  220.4 438.6 %all-gather.50.cloned.1.call-start = ((), (), s32[]{:S(2)}) async-start(), calls=%async_computation.29 | async-start | bytes 11280384 | tf_op jit(solution)/shard_map/all_gather | solution.py:42
  223.8 546.4 %all-gather.52.cloned.1.call-start = ((), (), s32[]{:S(2)}) async-start(), calls=%async_computation.30 | async-start | bytes 8146944 | tf_op jit(solution)/shard_map/all_gather | solution.py:42
  224.5 631.5 %all-gather.56.cloned.1.call-start = ((), (), s32[]{:S(2)}) async-start(), calls=%async_computation.32 | async-start | bytes 5013504 | tf_op jit(solution)/shard_map/all_gather | solution.py:71
  783.1 344.3 %all-gather.60.cloned.1.call-start = ((), (), s32[]{:S(2)}) async-start(), calls=%async_computation.34 | async-start | bytes 10653696 | tf_op jit(solution)/shard_map/all_gather | solution.py:42
  783.8 489.6 %all-gather.62.cloned.1.call-start = ((), (), s32[]{:S(2)}) async-start(), calls=%async_computation.35 | async-start | bytes 11280384 | tf_op jit(solution)/shard_map/all_gather | solution.py:42
  784.4 1478.0 %reduce-scatter.51.cloned.1.call-start = ((), (), s32[]{:S(2)}) async-start(), calls=%async_computation.20 | async-start | bytes 11280384 | tf_op jit(solution)/shard_map/reduce_scatter | solution.py:57
  1711.0 726.2 %reduce-scatter.53.cloned.1.call-start = ((), (), s32[]{:S(2)}) async-start(), calls=%async_computation.22 | async-start | bytes 11280384 | tf_op jit(solution)/shard_map/reduce_scatter | solution.py:57
  1722.6 881.4 %reduce-scatter.47.cloned.1.call-start = ((), (), s32[]{:S(2)}) async-start(), calls=%async_computation.18 | async-start | bytes 10653696 | tf_op jit(solution)/shard_map/reduce_scatter | solution.py:57
  1738.0 939.2 %reduce-scatter.71.cloned.1.call-start = ((), (), s32[]{:S(2)}) async-start(), calls=%async_computation.46 | async-start | bytes 2820096
  1749.2 1001.9 %reduce-scatter.73.cloned.1.call-start = ((), (), s32[]{:S(2)}) async-start(), calls=%async_computation.47 | async-start | bytes 2820096
  1752.6 1165.3 %reduce-scatter.49.cloned.1.call-start = ((), (), s32[]{:S(2)}) async-start(), calls=%async_computation.19 | async-start | bytes 10653696 | tf_op jit(solution)/shard_map/reduce_scatter | solution.py:57
  1764.9 1287.3 %reduce-scatter.43.cloned.1.call-start = ((), (), s32[]{:S(2)}) async-start(), calls=%async_computation.16 | async-start | bytes 8146944 | tf_op jit(solution)/shard_map/reduce_scatter | solution.py:57
  2216.4 970.1 %reduce-scatter.45.cloned.1.call-start = ((), (), s32[]{:S(2)}) async-start(), calls=%async_computation.17 | async-start | bytes 8146944 | tf_op jit(solution)/shard_map/reduce_scatter | solution.py:57
  2223.7 991.6 %reduce-scatter.67.cloned.1.call-start = ((), (), s32[]{:S(2)}) async-start(), calls=%async_computation.44 | async-start | bytes 1740800
  2265.0 994.6 %reduce-scatter.69.cloned.1.call-start = ((), (), s32[]{:S(2)}) async-start(), calls=%async_computation.45 | async-start | bytes 1740800
  2439.8 840.4 %reduce-scatter.63.cloned.1.call-start = ((), (), s32[]{:S(2)}) async-start(), calls=%async_computation.42 | async-start | bytes 2785280
  2607.6 696.7 %reduce-scatter.59.cloned.1.call-start = ((), (), s32[]{:S(2)}) async-start(), calls=%async_computation.40 | async-start | bytes 696320
  2679.2 649.7 %reduce-scatter.61.cloned.1.call-start = ((), (), s32[]{:S(2)}) async-start(), calls=%async_computation.41 | async-start | bytes 696320
  2753.1 611.3 %reduce-scatter.65.cloned.1.call-start = ((), (), s32[]{:S(2)}) async-start(), calls=%async_computation.43 | async-start | bytes 2785280
  2921.5 474.0 %reduce-scatter.55.cloned.1.call-start = ((), (), s32[]{:S(2)}) async-start(), calls=%async_computation.38 | async-start | bytes 2088960
  3054.9 372.9 %reduce-scatter.57.cloned.1.call-start = ((), (), s32[]{:S(2)}) async-start(), calls=%async_computation.39 | async-start | bytes 2088960
  3189.0 259.0 %all-gather.36.cloned.1.call-start = ((), (), s32[]{:S(2)}) async-start(), calls=%async_computation.21 | async-start | bytes 1740800 | tf_op jit(solution)/shard_map/all_gather | solution.py:335
  3215.3 252.8 %all-gather.38.cloned.1.call-start = ((), (), s32[]{:S(2)}) async-start(), calls=%async_computation.23 | async-start | bytes 1740800 | tf_op jit(solution)/shard_map/all_gather | solution.py:335
  (220 other events, 10484.9 us)
Sparse Core Ops, SparseCore 0:
  10.8 130.5 all-gather.39
  150.9 90.1 all-gather.43
  243.1 76.2 all-gather.41
  321.5 51.7 all-gather.45
  375.8 137.0 all-gather.47
  515.5 143.4 all-gather.49
  661.1 108.9 all-gather.51
  779.8 76.1 all-gather.55
  858.1 76.1 all-gather.53
  936.4 51.7 all-gather.57
  990.3 137.0 all-gather.59
  1130.0 143.4 all-gather.61
  1711.2 551.2 reduce-scatter.50
  2265.9 171.2 reduce-scatter.52
  2440.6 163.3 reduce-scatter.46
  2607.9 69.2 reduce-scatter.70
  2681.7 69.2 reduce-scatter.72
  2754.8 163.0 reduce-scatter.48
  2921.5 130.6 reduce-scatter.42
  3055.6 130.7 reduce-scatter.44
  3247.6 32.5 reduce-scatter.62
  3332.1 32.2 reduce-scatter.64
  3366.8 28.7 reduce-scatter.54
  3398.9 28.8 reduce-scatter.56
  (8 shorter events, 169.3 us)
where the time goes:
time: 3530 us; the launch traced here: 3520 us
  waiting for transfers between devices  2500 us (71%)
  matrix products  334 us (9%)
  blocking collectives  221 us (6%)
  starting transfers between devices  165 us (5%)
  local copies, waits for them, and re-layouts  160 us (5%)
  other arithmetic  122 us (3%)
    reduce_scatter x6, waiting for transfers between devices, weight_grad(): lax.psum_scatter(lax.dot_general(acts, grad, (((0,), (0,)), ((), ())), pr...  802 us
    all_gather x8, waiting for transfers between devices, forward_rows(): lax.all_gather(weight, 'shard', axis=0, tiled=True)  734 us
    ppermute x64, waiting for transfers between devices, passed_along(): return lax.ppermute(block, axis, route)  491 us
    unnamed x42, waiting for transfers between devices  277 us
    ppermute x64, starting transfers between devices, passed_along(): return lax.ppermute(block, axis, route)  163 us
    all_gather x2, waiting for transfers between devices, attend_forward(): lax.all_gather(values, 'shard', axis=1, tiled=True)  75.9 us
  transfers between devices with their start and end apart: 96, of which 91 were waited for; matrix products, arithmetic and copies ran while one was open for 15% of the time, Pallas kernels for 0%

commit v1 on v0

v1 whole, which is shorter than its diff:
```python
import jax
import jax.numpy as jnp
from jax import lax
from jax.sharding import PartitionSpec as P

HEADS = 17
HEAD_SIZE = 64
LAYERS = 2
SCALE = HEAD_SIZE ** (-0.5)

eps = 1e-05
masked = -1e30
low = jnp.bfloat16


def norm_forward(x, gain, bias):
    centre = jnp.mean(x, axis=-1, keepdims=True)
    centred = x - centre
    rstd = lax.rsqrt(jnp.mean(centred * centred, axis=-1, keepdims=True) + eps)
    normal = centred * rstd
    return (normal * gain + bias, (normal, rstd))


def norm_backward(grad, saved, gain):
    normal, rstd = saved
    scaled = grad * gain
    gain_grad = jnp.sum(grad * normal, axis=0)
    bias_grad = jnp.sum(grad, axis=0)
    inner = scaled - jnp.mean(scaled, axis=-1, keepdims=True)
    inner = inner - normal * jnp.mean(scaled * normal, axis=-1, keepdims=True)
    return (rstd * inner, gain_grad, bias_grad)


def dot(left, right, left_dim, right_dim):
    return lax.dot_general(
        left, right, (((left_dim,), (right_dim,)), ((), ())), preferred_element_type=jnp.float32
    )


def gather_tokens(block, seqs, span):
    whole = lax.all_gather(block.reshape(seqs, span, -1), "shard", axis=1, tiled=True)
    return whole.reshape(-1, block.shape[-1])


def scatter_tokens(partial, seqs):
    part = lax.psum_scatter(
        partial.astype(low).reshape(seqs, -1, partial.shape[-1]),
        "shard",
        scatter_dimension=1,
        tiled=True,
    )
    return part.reshape(-1, partial.shape[-1]).astype(jnp.float32)


def swap(blocks):
    return lax.all_to_all(blocks, "shard", split_axis=0, concat_axis=0, tiled=True)


def query_blocks(length):
    size = 512 if length % 512 == 0 else length
    return [(start, size) for start in range(0, length, size)]


def block_scores(query, keys, start, size):
    end = start + size
    scores = jnp.einsum("bqd,bkd->bqk", query, keys, preferred_element_type=jnp.float32) * SCALE
    query_pos = start + jnp.arange(size, dtype=jnp.int32)
    key_pos = jnp.arange(end, dtype=jnp.int32)
    return scores, (key_pos[None, :] <= query_pos[:, None])[None]


def attend_forward(query, keys, values):
    mixed, logsum = [], []
    for start, size in query_blocks(query.shape[1]):
        end = start + size
        scores, allowed = block_scores(query[:, start:end], keys[:, :end], start, size)
        scores = jnp.where(allowed, scores, masked)
        top = jnp.max(scores, axis=-1, keepdims=True)
        probs = jnp.exp(scores - top)
        total = jnp.sum(probs, axis=-1, keepdims=True)
        out = jnp.einsum(
            "bqk,bkd->bqd", probs.astype(low), values[:, :end], preferred_element_type=jnp.float32
        )
        mixed.append(out / total)
        logsum.append(top + jnp.log(total))
    return jnp.concatenate(mixed, axis=1), logsum


def attend_backward(query, keys, values, grad_out, logsum, delta):
    length = query.shape[1]
    query_grad = []
    key_grad = jnp.zeros(keys.shape, jnp.float32)
    value_grad = jnp.zeros(values.shape, jnp.float32)
    for block, (start, size) in enumerate(query_blocks(length)):
        end = start + size
        rows, cols = query[:, start:end], keys[:, :end]
        grad_rows = grad_out[:, start:end]
        scores, allowed = block_scores(rows, cols, start, size)
        probs = jnp.where(allowed, jnp.exp(scores - logsum[block]), 0.0)
        prob_grad = jnp.einsum(
            "bqd,bkd->bqk", grad_rows, values[:, :end], preferred_element_type=jnp.float32
        )
        score_grad = (probs * (prob_grad - delta[:, start:end]) * SCALE).astype(low)
        query_grad.append(
            jnp.einsum("bqk,bkd->bqd", score_grad, cols, preferred_element_type=jnp.float32)
        )
        key_add = jnp.einsum("bqk,bqd->bkd", score_grad, rows, preferred_element_type=jnp.float32)
        value_add = jnp.einsum(
            "bqk,bqd->bkd", probs.astype(low), grad_rows, preferred_element_type=jnp.float32
        )
        pad = ((0, 0), (0, length - end), (0, 0))
        key_grad = key_grad + jnp.pad(key_add, pad)
        value_grad = value_grad + jnp.pad(value_add, pad)
    return jnp.concatenate(query_grad, axis=1), key_grad, value_grad


def body(
    inputs, w_attn, w_out, w_fc, w_proj, norm_gains, norm_biases, dense_biases, fc_bias, cotangent
):
    seqs, span, width = inputs.shape
    count = lax.axis_size("shard")
    reps = lax.axis_size("rep")
    index = lax.axis_index("shard")
    length = span * count
    rows = w_attn.shape[1]
    own_heads = -(-HEADS // count)
    group = own_heads * HEAD_SIZE
    padded = group * count
    hidden_own = fc_bias.shape[1]

    def pad_last(array):
        return jnp.pad(array, [(0, 0)] * (array.ndim - 1) + [(0, padded - width)])

    def to_heads(flat):
        tensor = flat.reshape(seqs, length, own_heads, HEAD_SIZE).transpose(0, 2, 1, 3)
        return tensor.reshape(seqs * own_heads, length, HEAD_SIZE)

    def from_heads(tensor):
        flat = tensor.reshape(seqs, own_heads, length, HEAD_SIZE).transpose(0, 2, 1, 3)
        return flat.reshape(seqs * length, group)

    columns = []
    for layer in range(LAYERS):
        pieces = [
            pad_last(w_attn[layer][:, part * width : (part + 1) * width]).reshape(
                rows, count, group
            )
            for part in range(3)
        ]
        pieces.append(w_fc[layer].reshape(rows, count, hidden_own))
        send = jnp.concatenate(pieces, axis=2).transpose(1, 0, 2)
        columns.append(swap(send).reshape(rows * count, -1))

    vectors = jnp.concatenate([norm_gains, norm_biases, dense_biases], axis=1)
    vectors = lax.all_gather(vectors.reshape(LAYERS * 8, -1), "shard", axis=0, tiled=False)
    vectors = vectors.transpose(1, 0, 2).reshape(LAYERS, 8, width)
    vectors = lax.optimization_barrier(vectors)

    def own_part(vector):
        return lax.dynamic_slice_in_dim(pad_last(vector), index * group, group, 0)

    def spread(part):
        whole = lax.dynamic_update_slice_in_dim(
            jnp.zeros((padded,), part.dtype), part, index * group, 0
        )
        return whole[:width]

    state = inputs.reshape(seqs * span, width).astype(jnp.float32)
    stored = []
    for layer in range(LAYERS):
        vec = vectors[layer]
        attn_cols = columns[layer][:, : 3 * group]
        fc_cols = columns[layer][:, 3 * group :]
        out_full = lax.all_gather(w_out[layer], "shard", axis=0, tiled=True)
        normed, saved_one = norm_forward(state, vec[0], vec[2])
        normed_all = gather_tokens(normed.astype(low), seqs, span)
        mixed = dot(normed_all, attn_cols, 1, 0)
        query = to_heads((mixed[:, :group] + own_part(vec[4])).astype(low))
        keys = to_heads(mixed[:, group : 2 * group].astype(low))
        values = to_heads((mixed[:, 2 * group :] + own_part(vec[5])).astype(low))
        attended, logsum = attend_forward(query, keys, values)
        send = from_heads(attended.astype(low)).reshape(seqs, count, span, group)
        joined = swap(send.transpose(1, 0, 2, 3)).transpose(1, 2, 0, 3)
        attended_low = joined.reshape(seqs * span, padded)[:, :width]
        middle = state + dot(attended_low, out_full, 1, 0) + vec[6]
        normed2, saved_two = norm_forward(middle, vec[1], vec[3])
        normed2_all = gather_tokens(normed2.astype(low), seqs, span)
        hidden = dot(normed2_all, fc_cols, 1, 0) + fc_bias[layer]
        active_low = jax.nn.gelu(hidden, approximate=True).astype(low)
        state = middle + scatter_tokens(dot(active_low, w_proj[layer], 1, 0), seqs) + vec[7]
        stored.append(
            (
                attn_cols, fc_cols, out_full, saved_one, normed_all, query, keys, values,
                attended, logsum, attended_low, saved_two, normed2_all, hidden, active_low,
            )
        )
    result = state.reshape(seqs, span, width).astype(low)

    grad = cotangent.reshape(seqs * span, width).astype(jnp.float32)
    grads = [None] * LAYERS
    small = [None] * LAYERS
    fc_small = [None] * LAYERS
    for layer in reversed(range(LAYERS)):
        (
            attn_cols, fc_cols, out_full, saved_one, normed_all, query, keys, values,
            attended, logsum, attended_low, saved_two, normed2_all, hidden, active_low,
        ) = stored[layer]
        vec = vectors[layer]
        proj_bias_grad = jnp.sum(grad, axis=0)
        grad_all = gather_tokens(grad.astype(low), seqs, span)
        active_grad = dot(grad_all, w_proj[layer], 1, 1)
        gelu_pull = jax.vjp(lambda value: jax.nn.gelu(value, approximate=True), hidden)[1]
        hidden_grad = gelu_pull(active_grad)[0]
        fc_small[layer] = jnp.sum(hidden_grad, axis=0)
        hidden_low = hidden_grad.astype(low)
        normed2_grad = scatter_tokens(dot(hidden_low, fc_cols, 1, 1), seqs)
        proj_grad = dot(active_low, grad_all, 0, 0).astype(low)
        fc_grad = dot(normed2_all, hidden_low, 0, 0).astype(low)
        middle_norm, gain_two, shift_two = norm_backward(normed2_grad, saved_two, vec[1])
        middle_grad = grad + middle_norm
        out_bias_grad = jnp.sum(middle_grad, axis=0)
        middle_low = middle_grad.astype(low)
        attended_grad = pad_last(dot(middle_low, out_full, 1, 1).astype(low))
        send = attended_grad.reshape(seqs, span, count, group).transpose(2, 0, 1, 3)
        grad_heads = to_heads(swap(send).transpose(1, 0, 2, 3).reshape(seqs * length, group))
        out_grad = lax.psum_scatter(
            dot(attended_low, middle_low, 0, 0).astype(low),
            "shard",
            scatter_dimension=0,
            tiled=True,
        )
        delta = jnp.sum(grad_heads.astype(jnp.float32) * attended, axis=-1, keepdims=True)
        query_grad, key_grad, value_grad = attend_backward(
            query, keys, values, grad_heads, logsum, delta
        )
        query_bias = spread(jnp.sum(query_grad.reshape(seqs, own_heads, length, HEAD_SIZE), axis=(0, 2)).reshape(group))
        value_bias = spread(jnp.sum(value_grad.reshape(seqs, own_heads, length, HEAD_SIZE), axis=(0, 2)).reshape(group))
        mixed_low = jnp.concatenate(
            [from_heads(part.astype(low)) for part in (query_grad, key_grad, value_grad)], axis=1
        )
        normed_grad = scatter_tokens(dot(mixed_low, attn_cols, 1, 1), seqs)
        attn_grad = dot(normed_all, mixed_low, 0, 0).astype(low)
        input_norm, gain_one, shift_one = norm_backward(normed_grad, saved_one, vec[0])
        grad = middle_grad + input_norm

        small[layer] = jnp.stack(
            [gain_one, gain_two, shift_one, shift_two, query_bias, value_bias, out_bias_grad, proj_bias_grad]
        )
        by_cols = jnp.concatenate([attn_grad, fc_grad], axis=1)
        part_cols = by_cols.shape[1] // reps
        by_cols = by_cols.reshape(count * rows, reps, part_cols).transpose(1, 0, 2)
        by_cols = lax.psum_scatter(by_cols, "rep", scatter_dimension=0, tiled=False)
        by_cols = swap(by_cols.reshape(count, rows, part_cols))
        by_cols = lax.all_gather(by_cols, "rep", axis=0, tiled=False)
        by_cols = by_cols.transpose(2, 1, 0, 3).reshape(rows, count, reps * part_cols)
        attn_rows = [
            by_cols[:, :, part * group : (part + 1) * group].reshape(rows, padded)[:, :width]
            for part in range(3)
        ]
        attn_grad = jnp.concatenate(attn_rows, axis=1).astype(jnp.float32)
        fc_grad = by_cols[:, :, 3 * group :].reshape(rows, -1).astype(jnp.float32)
        by_rows = jnp.concatenate([proj_grad, out_grad], axis=0)
        by_rows = by_rows.reshape(-1, reps, width // reps).transpose(1, 0, 2)
        by_rows = lax.psum_scatter(by_rows, "rep", scatter_dimension=0, tiled=False)
        by_rows = lax.all_gather(by_rows, "rep", axis=0, tiled=False)
        by_rows = by_rows.transpose(1, 0, 2).reshape(-1, width).astype(jnp.float32)
        grads[layer] = (attn_grad, by_rows[hidden_own:], fc_grad, by_rows[:hidden_own])

    stacked = [jnp.stack([grads[layer][item] for layer in range(LAYERS)]) for item in range(4)]
    little = lax.psum(jnp.stack(small), ("rep", "shard"))
    little = lax.dynamic_slice_in_dim(little, index * rows, rows, 2)
    fc_little = lax.psum(jnp.stack(fc_small), "rep")
    return (
        result,
        grad.reshape(seqs, span, width),
        stacked[0],
        stacked[1],
        stacked[2],
        stacked[3],
        little[:, 0:2],
        little[:, 2:4],
        little[:, 4:8],
        fc_little,
    )


def solution(mesh):
    tokens = P("rep", "shard", None)
    weight = P(None, "shard", None)
    vector = P(None, None, "shard")
    in_specs = (
        tokens, weight, weight, weight, weight, vector, vector, vector, P(None, "shard"), tokens,
    )
    out_specs = (
        tokens, tokens, weight, weight, weight, weight, vector, vector, vector, P(None, "shard"),
    )
    return jax.shard_map(body, mesh=mesh, in_specs=in_specs, out_specs=out_specs, check_vma=False)
```

time: 3530 us -> 2050 us (0.58)
  waiting for transfers between devices: 2500 us -> 1420 us
  blocking collectives: 221 us -> 66.6 us
  starting transfers between devices: 165 us -> 34.7 us
  matrix products: 334 us -> 284 us
  other arithmetic: 122 us -> 80.5 us
    all_gather x16 -> x12, waiting for transfers between devices: 931 us -> 397 us  [the longest x6 307 us: gather_tokens(): lax.all_gather(block.reshape(seqs, span, -1), 'shard', axis=1, tiled=True)]
    ppermute x64 -> x0, waiting for transfers between devices: 491 us -> none  [passed_along(): return lax.ppermute(block, axis, route)]
    all_to_all x0 -> x7, waiting for transfers between devices: none -> 244 us  [swap(): lax.all_to_all(blocks, 'shard', split_axis=0, concat_axis=0, tiled=True)]
    unnamed x42 -> x27, waiting for transfers between devices: 277 us -> 61.1 us
    reduce_scatter x6 -> x10, waiting for transfers between devices: 802 us -> 619 us  [the longest x6 545 us: scatter_tokens(): lax.psum_scatter(partial.astype(low).reshape(seqs, -1, partial.shape[-1])...]
    ppermute x64 -> x0, starting transfers between devices: 163 us -> none  [passed_along(): return lax.ppermute(block, axis, route)]
    all_gather x8 -> x1, blocking collectives: 172 us -> 32.3 us  [body(): lax.all_gather(vectors.reshape(LAYERS * 8, -1), 'shard', axis=0, tiled=Fa...]
    psum x0 -> x1, waiting for transfers between devices: none -> 99.6 us  [body(): little = lax.psum(jnp.stack(small), ('rep', 'shard'))]
  transfers between devices with their start and end apart: 96 -> 32, of which waited for: 91 -> 28; matrix products, arithmetic and copies ran while one was open for 15% -> 16% of each run, Pallas kernels for 0% -> 0%
where the time goes in v1:
time: 2050 us; the launch traced here: 2040 us
  waiting for transfers between devices  1420 us (69%)
  matrix products  284 us (14%)
  local copies, waits for them, and re-layouts  134 us (7%)
  other arithmetic  80.5 us (4%)
  blocking collectives  66.6 us (3%)
  starting transfers between devices  34.7 us (2%)
    reduce_scatter x6, waiting for transfers between devices, scatter_tokens(): lax.psum_scatter(partial.astype(low).reshape(seqs, -1, partial.shape[-1])...  545 us
    all_gather x6, waiting for transfers between devices, gather_tokens(): lax.all_gather(block.reshape(seqs, span, -1), 'shard', axis=1, tiled=True)  307 us
    all_to_all x7, waiting for transfers between devices, swap(): lax.all_to_all(blocks, 'shard', split_axis=0, concat_axis=0, tiled=True)  244 us
    dot_general x24, matrix products, dot(): lax.dot_general(left, right, (((left_dim,), (right_dim,)), ((), ())), pre...  142 us
    psum x1, waiting for transfers between devices, body(): little = lax.psum(jnp.stack(small), ('rep', 'shard'))  99.6 us
    reduce_scatter x2, waiting for transfers between devices, body(): by_cols = lax.psum_scatter(by_cols, 'rep', scatter_dimension=0, tiled=False)  70.1 us
    unnamed x27, waiting for transfers between devices  61.1 us
    all_gather x2, waiting for transfers between devices, body(): by_cols = lax.all_gather(by_cols, 'rep', axis=0, tiled=False)  55.2 us
  transfers between devices with their start and end apart: 32, of which 28 were waited for; matrix products, arithmetic and copies ran while one was open for 16% of the time, Pallas kernels for 0%

profile of v1, /device:TPU:0, one launch (start us, length us, event | category | flops | bytes accessed | tf_op | source)
XLA Modules:
  0.0 2037.5 jit_solution(5521572802677410210)
XLA Ops:
  10.5 32.3 %all_gather.45 = f32[8,16,136]{2,1,0:T(8,128)S(1)} all-gather(f32[1,16,136]{2,1,0:T(8,128)S(1)} %maximum_bitcast_fusion), channel_id=1, replica_groups=mesh['rep'=4,'shard'=8] {'shard'}, dimensions={0}, use_global_device_ids=true | all-gather | bytes 78336 | tf_op jit(solution)/shard_map/all_gather | solution.py:155
  73.2 92.4 %all-to-all-done = bf16[8,136,1120]{2,1,0:T(8,128)(2,1)} async-done(((bf16[8,136,1120]{2,1,0:T(8,128)(2,1)}), bf16[8,136,1120]{2,1,0:T(8,128)(2,1)}, u32[]{:S(2)}, u32[]{:S(2)}) %all-to-all-start) | async-done | bytes 2437152 | tf_op jit(solution)/shard_map/all_to_all | solution.py:56
  226.1 14.9 all-to-all-done.1
  247.1 75.6 %all-gather.31.cloned.1.call-done = bf16[2048,1088]{0,1:T(8,128)(2,1)} async-done(((bf16[256,1088]{0,1:T(8,128)(2,1)}), bf16[2048,1088]{0,1:T(8,128)(2,1)}) %all-gather.31.cloned.1.call-update) | async-done | bytes 4456464 | tf_op jit(solution)/shard_map/all_gather | solution.py:41
  337.9 90.5 %reduce-scatter.17.cloned.1.call-done = bf16[1,256,1088]{1,2,0:T(8,128)(2,1)} async-done(((bf16[1,2048,1088]{1,2,0:T(8,128)(2,1)}), bf16[1,256,1088]{1,2,0:T(8,128)(2,1)}) %reduce-scatter.17.cloned.1.call-update) | async-done | bytes 557072 | tf_op jit(solution)/shard_map/reduce_scatter | solution.py:46
  457.7 92.2 %all-to-all-done.2 = bf16[8,136,1120]{2,1,0:T(8,128)(2,1)} async-done(((bf16[8,136,1120]{2,1,0:T(8,128)(2,1)}), bf16[8,136,1120]{2,1,0:T(8,128)(2,1)}, u32[]{:S(2)}, u32[]{:S(2)}) %all-to-all-start.2) | async-done | bytes 2437152 | tf_op jit(solution)/shard_map/all_to_all | solution.py:56
  612.4 15.0 all-to-all-done.3
  633.1 75.2 %all-gather.37.cloned.1.call-done = bf16[2048,1088]{0,1:T(8,128)(2,1)} async-done(((bf16[256,1088]{0,1:T(8,128)(2,1)}), bf16[2048,1088]{0,1:T(8,128)(2,1)}) %all-gather.37.cloned.1.call-update) | async-done | bytes 4456464 | tf_op jit(solution)/shard_map/all_gather | solution.py:41
  716.3 70.4 %all-gather.23.cloned.1.call-done = bf16[1,2048,1088]{1,2,0:T(8,128)(2,1)} async-done(((bf16[1,256,1088]{1,2,0:T(8,128)(2,1)}), bf16[1,2048,1088]{1,2,0:T(8,128)(2,1)}) %all-gather.23.cloned.1.call-update) | async-done | bytes 4456464 | tf_op jit(solution)/shard_map/all_gather | solution.py:41
  813.8 80.8 %reduce-scatter.21.cloned.1.call-done = bf16[1,256,1088]{1,2,0:T(8,128)(2,1)} async-done(((bf16[1,2048,1088]{1,2,0:T(8,128)(2,1)}), bf16[1,256,1088]{1,2,0:T(8,128)(2,1)}) %reduce-scatter.21.cloned.1.call-update) | async-done | bytes 557072 | tf_op jit(solution)/shard_map/reduce_scatter | solution.py:46
  896.9 93.0 %reduce-scatter.19.cloned.1.call-done = bf16[1,256,1088]{1,2,0:T(8,128)(2,1)} async-done(((bf16[1,2048,1088]{1,2,0:T(8,128)(2,1)}), bf16[1,256,1088]{1,2,0:T(8,128)(2,1)}) %reduce-scatter.19.cloned.1.call-update) | async-done | bytes 557072 | tf_op jit(solution)/shard_map/reduce_scatter | solution.py:46
  1000.0 20.1 all-to-all-done.4
  1082.4 91.1 %reduce-scatter.23.cloned.1.call-done = bf16[1,256,1088]{1,2,0:T(8,128)(2,1)} async-done(((bf16[1,2048,1088]{1,2,0:T(8,128)(2,1)}), bf16[1,256,1088]{1,2,0:T(8,128)(2,1)}) %reduce-scatter.23.cloned.1.call-update) | async-done | bytes 557072 | tf_op jit(solution)/shard_map/reduce_scatter | solution.py:46
  1178.1 77.5 %all-gather.39.cloned.1.call-done = bf16[2048,1088]{0,1:T(8,128)(2,1)} async-done(((bf16[256,1088]{0,1:T(8,128)(2,1)}), bf16[2048,1088]{0,1:T(8,128)(2,1)}) %all-gather.39.cloned.1.call-update) | async-done | bytes 4456464 | tf_op jit(solution)/shard_map/all_gather | solution.py:41
  1276.8 86.9 %reduce-scatter.25.cloned.1.call-done = bf16[1,256,1088]{1,2,0:T(8,128)(2,1)} async-done(((bf16[1,2048,1088]{1,2,0:T(8,128)(2,1)}), bf16[1,256,1088]{1,2,0:T(8,128)(2,1)}) %reduce-scatter.25.cloned.1.call-update) | async-done | bytes 557072 | tf_op jit(solution)/shard_map/reduce_scatter | solution.py:46
  1379.6 58.8 %reduce-scatter.39.cloned.1.call-done = bf16[136,1088]{1,0:T(8,128)(2,1)} async-done(((bf16[1088,1088]{1,0:T(8,128)(2,1)}), bf16[136,1088]{1,0:T(8,128)(2,1)}) %reduce-scatter.39.cloned.1.call-update) | async-done | bytes 295952
  1562.3 30.0 %reduce-scatter.31.cloned.1.call-done = bf16[1,1088,280]{2,1,0:T(8,128)(2,1)} async-done(((bf16[4,1088,280]{2,1,0:T(8,128)(2,1)}), bf16[1,1088,280]{2,1,0:T(8,128)(2,1)}) %reduce-scatter.31.cloned.1.call-update) | async-done | bytes 609296 | tf_op jit(solution)/shard_map/reduce_scatter | solution.py:252
  1592.4 27.5 %all_to_all.40 = bf16[8,136,280]{2,1,0:T(8,128)(2,1)} all-to-all(bf16[8,136,280]{2,1,0:T(8,128)(2,1)} %bitcast.531), channel_id=1, replica_groups=mesh['rep'=4,'shard'=8] {'shard'}, dimensions={0} | all-to-all | bytes 1218560 | tf_op jit(solution)/shard_map/all_to_all | solution.py:56
  1626.0 40.1 %reduce-scatter.29.cloned.1.call-done = bf16[1,1088,280]{2,1,0:T(8,128)(2,1)} async-done(((bf16[4,1088,280]{2,1,0:T(8,128)(2,1)}), bf16[1,1088,280]{2,1,0:T(8,128)(2,1)}) %reduce-scatter.29.cloned.1.call-update) | async-done | bytes 609296 | tf_op jit(solution)/shard_map/reduce_scatter | solution.py:252
  1672.1 102.6 %reduce-scatter.27.cloned.1.call-done = bf16[1,256,1088]{1,2,0:T(8,128)(2,1)} async-done(((bf16[1,2048,1088]{1,2,0:T(8,128)(2,1)}), bf16[1,256,1088]{1,2,0:T(8,128)(2,1)}) %reduce-scatter.27.cloned.1.call-update) | async-done | bytes 557072 | tf_op jit(solution)/shard_map/reduce_scatter | solution.py:46
  1778.4 17.8 all-gather.27.cloned.1.call-done
  1802.4 25.0 %all-gather.43.cloned.1.call-done = bf16[32,136,280]{2,1,0:T(8,128)(2,1)} async-done(((bf16[8,136,280]{2,1,0:T(8,128)(2,1)}), bf16[32,136,280]{2,1,0:T(8,128)(2,1)}) %all-gather.43.cloned.1.call-update) | async-done | bytes 2437136 | tf_op jit(solution)/shard_map/all_gather | solution.py:254
  1873.4 99.6 %all-reduce.26.cloned.1.call-done = f32[2,8,1088]{2,1,0:T(8,128)} async-done(((f32[2,8,1088]{2,1,0:T(8,128)}), f32[2,8,1088]{2,1,0:T(8,128)}) %all-reduce.26.cloned.1.call-update) | async-done | bytes 69648 | tf_op jit(solution)/shard_map/psum | solution.py:270
  1976.0 30.2 %all-gather.41.cloned.1.call-done = bf16[32,136,280]{2,1,0:T(8,128)(2,1)} async-done(((bf16[8,136,280]{2,1,0:T(8,128)(2,1)}), bf16[32,136,280]{2,1,0:T(8,128)(2,1)}) %all-gather.41.cloned.1.call-update) | async-done | bytes 2437136 | tf_op jit(solution)/shard_map/all_gather | solution.py:254
  (726 shorter events, 580.7 us)
Async XLA Ops:
  7.2 162.0 %all-gather.21.cloned.1.call-start = ((), (), s32[]{:S(2)}) async-start(), calls=%async_computation.20 | async-start | bytes 5013504 | tf_op jit(solution)/shard_map/all_gather | solution.py:41
  70.4 155.7 %all-gather.29.cloned.1.call-start = ((), (), s32[]{:S(2)}) async-start(), calls=%async_computation.35 | async-start | bytes 2820096 | tf_op jit(solution)/shard_map/all_gather | solution.py:174
  246.5 181.9 %reduce-scatter.17.cloned.1.call-start = ((), (), s32[]{:S(2)}) async-start(), calls=%async_computation.21 | async-start | bytes 5013504 | tf_op jit(solution)/shard_map/reduce_scatter | solution.py:46
  337.9 216.5 %all-gather.33.cloned.1.call-start = ((), (), s32[]{:S(2)}) async-start(), calls=%async_computation.37 | async-start | bytes 5013504 | tf_op jit(solution)/shard_map/all_gather | solution.py:41
  457.0 155.4 %all-gather.35.cloned.1.call-start = ((), (), s32[]{:S(2)}) async-start(), calls=%async_computation.38 | async-start | bytes 2820096 | tf_op jit(solution)/shard_map/all_gather | solution.py:174
  632.1 154.7 %all-gather.23.cloned.1.call-start = ((), (), s32[]{:S(2)}) async-start(), calls=%async_computation.23 | async-start | bytes 5013504 | tf_op jit(solution)/shard_map/all_gather | solution.py:41
  632.8 261.8 %reduce-scatter.21.cloned.1.call-start = ((), (), s32[]{:S(2)}) async-start(), calls=%async_computation.24 | async-start | bytes 5013504 | tf_op jit(solution)/shard_map/reduce_scatter | solution.py:46
  804.3 185.6 %reduce-scatter.19.cloned.1.call-start = ((), (), s32[]{:S(2)}) async-start(), calls=%async_computation.22 | async-start | bytes 5013504 | tf_op jit(solution)/shard_map/reduce_scatter | solution.py:46
  999.7 173.8 %reduce-scatter.23.cloned.1.call-start = ((), (), s32[]{:S(2)}) async-start(), calls=%async_computation.25 | async-start | bytes 5013504 | tf_op jit(solution)/shard_map/reduce_scatter | solution.py:46
  1082.3 173.2 %all-gather.39.cloned.1.call-start = ((), (), s32[]{:S(2)}) async-start(), calls=%async_computation.40 | async-start | bytes 5013504 | tf_op jit(solution)/shard_map/all_gather | solution.py:41
  1177.6 186.0 %reduce-scatter.25.cloned.1.call-start = ((), (), s32[]{:S(2)}) async-start(), calls=%async_computation.26 | async-start | bytes 5013504 | tf_op jit(solution)/shard_map/reduce_scatter | solution.py:46
  1273.2 165.3 %reduce-scatter.39.cloned.1.call-start = ((), (), s32[]{:S(2)}) async-start(), calls=%async_computation.44 | async-start | bytes 2820096
  1276.8 253.4 %reduce-scatter.37.cloned.1.call-start = ((), (), s32[]{:S(2)}) async-start(), calls=%async_computation.43 | async-start | bytes 2820096
  1371.5 190.1 %reduce-scatter.35.cloned.1.call-start = ((), (), s32[]{:S(2)}) async-start(), calls=%async_computation.32 | async-start | bytes 2088960 | tf_op jit(solution)/shard_map/reduce_scatter | solution.py:264
  1442.0 150.4 %reduce-scatter.31.cloned.1.call-start = ((), (), s32[]{:S(2)}) async-start(), calls=%async_computation.29 | async-start | bytes 4177920 | tf_op jit(solution)/shard_map/reduce_scatter | solution.py:252
  1465.5 158.3 %reduce-scatter.33.cloned.1.call-start = ((), (), s32[]{:S(2)}) async-start(), calls=%async_computation.30 | async-start | bytes 2088960 | tf_op jit(solution)/shard_map/reduce_scatter | solution.py:264
  1534.1 132.0 %reduce-scatter.29.cloned.1.call-start = ((), (), s32[]{:S(2)}) async-start(), calls=%async_computation.28 | async-start | bytes 4177920 | tf_op jit(solution)/shard_map/reduce_scatter | solution.py:252
  1553.3 221.3 %reduce-scatter.27.cloned.1.call-start = ((), (), s32[]{:S(2)}) async-start(), calls=%async_computation.27 | async-start | bytes 5013504 | tf_op jit(solution)/shard_map/reduce_scatter | solution.py:46
  1561.6 234.6 %all-gather.27.cloned.1.call-start = ((), (), s32[]{:S(2)}) async-start(), calls=%async_computation.33 | async-start | bytes 2088960 | tf_op jit(solution)/shard_map/all_gather | solution.py:265
  1562.3 265.1 %all-gather.43.cloned.1.call-start = ((), (), s32[]{:S(2)}) async-start(), calls=%async_computation.42 | async-start | bytes 4177920 | tf_op jit(solution)/shard_map/all_gather | solution.py:254
  1619.9 235.7 %all-gather.25.cloned.1.call-start = ((), (), s32[]{:S(2)}) async-start(), calls=%async_computation.31 | async-start | bytes 2088960 | tf_op jit(solution)/shard_map/all_gather | solution.py:265
  1666.1 176.0 %all-to-all-start.6 = ((bf16[8,136,280]{2,1,0:T(8,128)(2,1)}), bf16[8,136,280]{2,1,0:T(8,128)(2,1)}, u32[]{:S(2)}, u32[]{:S(2)}) async-start(bf16[8,136,280]{2,1,0:T(8,128)(2,1)} %bitcast.530), calls=%async_computation.13 | async-start | bytes 1671168 | tf_op jit(solution)/shard_map/all_to_all | solution.py:56
  1671.7 301.4 %all-reduce.26.cloned.1.call-start = ((), (), s32[]{:S(2)}) async-start(), calls=%async_computation.34 | async-start | bytes 147456 | tf_op jit(solution)/shard_map/psum | solution.py:270
  1778.4 227.8 %all-gather.41.cloned.1.call-start = ((), (), s32[]{:S(2)}) async-start(), calls=%async_computation.41 | async-start | bytes 4177920 | tf_op jit(solution)/shard_map/all_gather | solution.py:254
  (195 other events, 6663.5 us)
Sparse Core Ops, SparseCore 0:
  46.7 122.4 all-gather.20
  172.0 54.0 all-gather.28
  246.6 76.0 all-gather.30
  338.0 90.3 reduce-scatter.16
  431.3 123.1 all-gather.32
  556.7 55.6 all-gather.34
  632.2 76.0 all-gather.36
  710.5 76.1 all-gather.22
  804.4 90.1 reduce-scatter.20
  898.1 91.7 reduce-scatter.18
  1082.5 90.9 reduce-scatter.22
  1177.7 77.7 all-gather.38
  1273.2 90.3 reduce-scatter.24
  1368.2 70.2 reduce-scatter.38
  1442.9 76.9 reduce-scatter.36
  1522.5 27.6 reduce-scatter.34
  1553.2 39.1 reduce-scatter.30
  1594.9 28.7 reduce-scatter.32
  1626.9 39.1 reduce-scatter.28
  1670.6 103.9 reduce-scatter.26
  1797.7 29.6 all-gather.42
  1829.0 20.1 all-gather.24
  1854.7 118.3 all-reduce.25
  1974.6 31.5 all-gather.40
  (1 shorter events, 19.9 us)

commit v2 on v1

--- a/solution.py
+++ b/solution.py
@@ -40,6 +40,19 @@
 def gather_tokens(block, seqs, span):
     whole = lax.all_gather(block.reshape(seqs, span, -1), "shard", axis=1, tiled=True)
     return whole.reshape(-1, block.shape[-1])
+
+
+def gather_reps(block):
+    return lax.all_gather(block, "rep", axis=0, tiled=True)
+
+
+def scatter_reps(partial):
+    part = lax.psum_scatter(partial.astype(low), "rep", scatter_dimension=0, tiled=True)
+    return part.astype(jnp.float32)
+
+
+def scatter_rows(partial):
+    return lax.psum_scatter(partial.astype(low), "shard", scatter_dimension=0, tiled=True)
 
 
 def scatter_tokens(partial, seqs):
@@ -126,7 +139,9 @@
     own_heads = -(-HEADS // count)
     group = own_heads * HEAD_SIZE
     padded = group * count
-    hidden_own = fc_bias.shape[1]
+    replica = lax.axis_index("rep")
+    hidden_own = fc_bias.shape[1] // reps
+    quarter = 3 * group // reps
 
     def pad_last(array):
         return jnp.pad(array, [(0, 0)] * (array.ndim - 1) + [(0, padded - width)])
@@ -138,6 +153,16 @@
     def from_heads(tensor):
         flat = tensor.reshape(seqs, own_heads, length, HEAD_SIZE).transpose(0, 2, 1, 3)
         return flat.reshape(seqs * length, group)
+
+    def of_replica(array, axis, size):
+        return lax.dynamic_slice_in_dim(array, replica * size, size, axis)
+
+    vectors = jnp.concatenate(
+        [norm_gains, norm_biases, dense_biases, of_replica(fc_bias, 1, hidden_own)[:, None]], axis=1
+    )
+    vectors = lax.all_gather(vectors.reshape(LAYERS * 9, -1), "shard", axis=0, tiled=False)
+    vectors = vectors.transpose(1, 0, 2).reshape(LAYERS, 9, width)
+    vectors = lax.optimization_barrier(vectors)
 
     columns = []
     for layer in range(LAYERS):
@@ -147,14 +172,18 @@
             )
             for part in range(3)
         ]
-        pieces.append(w_fc[layer].reshape(rows, count, hidden_own))
         send = jnp.concatenate(pieces, axis=2).transpose(1, 0, 2)
-        columns.append(swap(send).reshape(rows * count, -1))
-
-    vectors = jnp.concatenate([norm_gains, norm_biases, dense_biases], axis=1)
-    vectors = lax.all_gather(vectors.reshape(LAYERS * 8, -1), "shard", axis=0, tiled=False)
-    vectors = vectors.transpose(1, 0, 2).reshape(LAYERS, 8, width)
-    vectors = lax.optimization_barrier(vectors)
+        mine = lax.all_gather(swap(of_replica(send, 2, quarter)), "rep", axis=0, tiled=False)
+        attn_cols = mine.transpose(1, 2, 0, 3).reshape(rows * count, 3 * group)
+        fc_part = of_replica(w_fc[layer].reshape(rows, count, -1), 2, hidden_own)
+        fc_cols = lax.all_gather(
+            fc_part.reshape(rows, count * hidden_own), "shard", axis=0, tiled=True
+        )
+        proj_rows = lax.all_gather(
+            of_replica(w_proj[layer], 0, hidden_own), "shard", axis=0, tiled=True
+        )
+        out_full = lax.all_gather(w_out[layer], "shard", axis=0, tiled=True)
+        columns.append((attn_cols, out_full, fc_cols, proj_rows))
 
     def own_part(vector):
         return lax.dynamic_slice_in_dim(pad_last(vector), index * group, group, 0)
@@ -169,9 +198,7 @@
     stored = []
     for layer in range(LAYERS):
         vec = vectors[layer]
-        attn_cols = columns[layer][:, : 3 * group]
-        fc_cols = columns[layer][:, 3 * group :]
-        out_full = lax.all_gather(w_out[layer], "shard", axis=0, tiled=True)
+        attn_cols, out_full, fc_cols, proj_rows = columns[layer]
         normed, saved_one = norm_forward(state, vec[0], vec[2])
         normed_all = gather_tokens(normed.astype(low), seqs, span)
         mixed = dot(normed_all, attn_cols, 1, 0)
@@ -184,13 +211,13 @@
         attended_low = joined.reshape(seqs * span, padded)[:, :width]
         middle = state + dot(attended_low, out_full, 1, 0) + vec[6]
         normed2, saved_two = norm_forward(middle, vec[1], vec[3])
-        normed2_all = gather_tokens(normed2.astype(low), seqs, span)
-        hidden = dot(normed2_all, fc_cols, 1, 0) + fc_bias[layer]
+        normed2_all = gather_reps(normed2.astype(low))
+        hidden = dot(normed2_all, fc_cols, 1, 0) + vec[8]
         active_low = jax.nn.gelu(hidden, approximate=True).astype(low)
-        state = middle + scatter_tokens(dot(active_low, w_proj[layer], 1, 0), seqs) + vec[7]
+        state = middle + scatter_reps(dot(active_low, proj_rows, 1, 0)) + vec[7]
         stored.append(
             (
-                attn_cols, fc_cols, out_full, saved_one, normed_all, query, keys, values,
+                saved_one, normed_all, query, keys, values,
                 attended, logsum, attended_low, saved_two, normed2_all, hidden, active_low,
             )
         )
@@ -199,23 +226,23 @@
     grad = cotangent.reshape(seqs * span, width).astype(jnp.float32)
     grads = [None] * LAYERS
     small = [None] * LAYERS
-    fc_small = [None] * LAYERS
     for layer in reversed(range(LAYERS)):
         (
-            attn_cols, fc_cols, out_full, saved_one, normed_all, query, keys, values,
+            saved_one, normed_all, query, keys, values,
             attended, logsum, attended_low, saved_two, normed2_all, hidden, active_low,
         ) = stored[layer]
+        attn_cols, out_full, fc_cols, proj_rows = columns[layer]
         vec = vectors[layer]
         proj_bias_grad = jnp.sum(grad, axis=0)
-        grad_all = gather_tokens(grad.astype(low), seqs, span)
-        active_grad = dot(grad_all, w_proj[layer], 1, 1)
+        grad_all = gather_reps(grad.astype(low))
+        active_grad = dot(grad_all, proj_rows, 1, 1)
         gelu_pull = jax.vjp(lambda value: jax.nn.gelu(value, approximate=True), hidden)[1]
         hidden_grad = gelu_pull(active_grad)[0]
-        fc_small[layer] = jnp.sum(hidden_grad, axis=0)
+        fc_bias_grad = jnp.sum(hidden_grad, axis=0)
         hidden_low = hidden_grad.astype(low)
-        normed2_grad = scatter_tokens(dot(hidden_low, fc_cols, 1, 1), seqs)
-        proj_grad = dot(active_low, grad_all, 0, 0).astype(low)
-        fc_grad = dot(normed2_all, hidden_low, 0, 0).astype(low)
+        normed2_grad = scatter_reps(dot(hidden_low, fc_cols, 1, 1))
+        proj_grad = scatter_rows(dot(active_low, grad_all, 0, 0))
+        fc_grad = scatter_rows(dot(normed2_all, hidden_low, 0, 0))
         middle_norm, gain_two, shift_two = norm_backward(normed2_grad, saved_two, vec[1])
         middle_grad = grad + middle_norm
         out_bias_grad = jnp.sum(middle_grad, axis=0)
@@ -223,12 +250,7 @@
         attended_grad = pad_last(dot(middle_low, out_full, 1, 1).astype(low))
         send = attended_grad.reshape(seqs, span, count, group).transpose(2, 0, 1, 3)
         grad_heads = to_heads(swap(send).transpose(1, 0, 2, 3).reshape(seqs * length, group))
-        out_grad = lax.psum_scatter(
-            dot(attended_low, middle_low, 0, 0).astype(low),
-            "shard",
-            scatter_dimension=0,
-            tiled=True,
-        )
+        out_grad = dot(attended_low, middle_low, 0, 0).astype(low)
         delta = jnp.sum(grad_heads.astype(jnp.float32) * attended, axis=-1, keepdims=True)
         query_grad, key_grad, value_grad = attend_backward(
             query, keys, values, grad_heads, logsum, delta
@@ -244,32 +266,44 @@
         grad = middle_grad + input_norm
 
         small[layer] = jnp.stack(
-            [gain_one, gain_two, shift_one, shift_two, query_bias, value_bias, out_bias_grad, proj_bias_grad]
-        )
-        by_cols = jnp.concatenate([attn_grad, fc_grad], axis=1)
-        part_cols = by_cols.shape[1] // reps
-        by_cols = by_cols.reshape(count * rows, reps, part_cols).transpose(1, 0, 2)
-        by_cols = lax.psum_scatter(by_cols, "rep", scatter_dimension=0, tiled=False)
-        by_cols = swap(by_cols.reshape(count, rows, part_cols))
-        by_cols = lax.all_gather(by_cols, "rep", axis=0, tiled=False)
-        by_cols = by_cols.transpose(2, 1, 0, 3).reshape(rows, count, reps * part_cols)
+            [gain_one, gain_two, shift_one, shift_two, query_bias, value_bias, out_bias_grad, proj_bias_grad, fc_bias_grad]
+        )
+        both = jnp.concatenate(
+            [
+                attn_grad.reshape(width, reps, quarter),
+                out_grad.reshape(width, reps, width // reps),
+            ],
+            axis=2,
+        ).transpose(1, 0, 2)
+        both = lax.psum_scatter(both, "rep", scatter_dimension=0, tiled=False)
+        attn_part = swap(both[:, :quarter].reshape(count, rows, quarter))
+        attn_part = attn_part.transpose(1, 0, 2).reshape(rows, count * quarter)
+        out_part = lax.psum_scatter(
+            both[:, quarter:], "shard", scatter_dimension=0, tiled=True
+        )
+        early = lax.all_gather(jnp.stack([proj_grad.reshape(-1), fc_grad.reshape(-1)]), "rep", axis=0)
+        proj_grad = early[:, 0].reshape(reps * hidden_own, width).astype(jnp.float32)
+        fc_grad = early[:, 1].reshape(reps, rows, count, hidden_own).transpose(1, 2, 0, 3)
+        fc_grad = fc_grad.reshape(rows, -1).astype(jnp.float32)
+        late = lax.all_gather(jnp.concatenate([attn_part, out_part], axis=1), "rep", axis=0)
+        out_grad = late[:, :, count * quarter :].transpose(1, 0, 2).reshape(rows, width)
+        by_heads = late[:, :, : count * quarter].reshape(reps, rows, count, quarter)
+        by_heads = by_heads.transpose(1, 2, 0, 3).reshape(rows, count, 3 * group)
         attn_rows = [
-            by_cols[:, :, part * group : (part + 1) * group].reshape(rows, padded)[:, :width]
+            by_heads[:, :, part * group : (part + 1) * group].reshape(rows, padded)[:, :width]
             for part in range(3)
         ]
         attn_grad = jnp.concatenate(attn_rows, axis=1).astype(jnp.float32)
-        fc_grad = by_cols[:, :, 3 * group :].reshape(rows, -1).astype(jnp.float32)
-        by_rows = jnp.concatenate([proj_grad, out_grad], axis=0)
-        by_rows = by_rows.reshape(-1, reps, width // reps).transpose(1, 0, 2)
-        by_rows = lax.psum_scatter(by_rows, "rep", scatter_dimension=0, tiled=False)
-        by_rows = lax.all_gather(by_rows, "rep", axis=0, tiled=False)
-        by_rows = by_rows.transpose(1, 0, 2).reshape(-1, width).astype(jnp.float32)
-        grads[layer] = (attn_grad, by_rows[hidden_own:], fc_grad, by_rows[:hidden_own])
+        grads[layer] = (attn_grad, out_grad.astype(jnp.float32), fc_grad, proj_grad)
 
     stacked = [jnp.stack([grads[layer][item] for layer in range(LAYERS)]) for item in range(4)]
-    little = lax.psum(jnp.stack(small), ("rep", "shard"))
-    little = lax.dynamic_slice_in_dim(little, index * rows, rows, 2)
-    fc_little = lax.psum(jnp.stack(fc_small), "rep")
+    little = jnp.stack(small).reshape(LAYERS * 9, count, rows).transpose(1, 0, 2)
+    little = jnp.sum(swap(little), axis=0).reshape(LAYERS, 9, rows)
+    fc_little = lax.dynamic_update_slice_in_dim(
+        jnp.zeros((LAYERS, reps, rows), jnp.float32), little[:, 8:], replica, 1
+    )
+    little = lax.psum(jnp.concatenate([little[:, :8], fc_little], axis=1), "rep")
+    fc_little = little[:, 8:].reshape(LAYERS, reps * rows)
     return (
         result,
         grad.reshape(seqs, span, width),

time: 2050 us -> 1820 us (0.89)
  waiting for transfers between devices: 1420 us -> 1040 us
  local copies, waits for them, and re-layouts: 134 us -> 244 us
  blocking collectives: 66.6 us -> 102 us
    reduce_scatter x6 -> x2, waiting for transfers between devices: 545 us -> 144 us  [scatter_tokens(): lax.psum_scatter(partial.astype(low).reshape(seqs, -1, partial.shape[-1])...]
    all_gather x4 -> x14, waiting for transfers between devices: 73 us -> 270 us  [the longest x2 105 us: body(): lax.all_gather(of_replica(w_proj[layer], 0, hidden_own), 'shard', axis=0,...]
    unnamed x27 -> x38, waiting for transfers between devices: 61.1 us -> 244 us
    all_gather x6 -> x2, waiting for transfers between devices: 307 us -> 131 us  [gather_tokens(): lax.all_gather(block.reshape(seqs, span, -1), 'shard', axis=1, tiled=True)]
    all_to_all x7 -> x6, waiting for transfers between devices: 244 us -> 81.4 us  [swap(): lax.all_to_all(blocks, 'shard', split_axis=0, concat_axis=0, tiled=True)]
    psum x1 -> x0, waiting for transfers between devices: 99.6 us -> none  [body(): little = lax.psum(jnp.stack(small), ('rep', 'shard'))]
    reduce_scatter x4 -> x6, waiting for transfers between devices: 73.9 us -> 151 us  [the longest x4 88.8 us: scatter_reps(): lax.psum_scatter(partial.astype(low), 'rep', scatter_dimension=0, tiled=T...]
    slice x13 -> x16, local copies, waits for them, and re-layouts: 17.4 us -> 76.8 us  [the longest x2 56.3 us: body(): early[:, 0].reshape(reps * hidden_own, width).astype(jnp.float32)]
  transfers between devices with their start and end apart: 32 -> 38, of which waited for: 28 -> 30; matrix products, arithmetic and copies ran while one was open for 16% -> 27% of each run, Pallas kernels for 0% -> 0%
where the time goes in v2:
time: 1820 us; the launch traced here: 1810 us
  waiting for transfers between devices  1040 us (57%)
  matrix products  278 us (15%)
  local copies, waits for them, and re-layouts  244 us (13%)
  blocking collectives  102 us (6%)
  other arithmetic  96.6 us (5%)
  starting transfers between devices  30.5 us (2%)
    unnamed x38, waiting for transfers between devices  244 us
    reduce_scatter x2, waiting for transfers between devices, scatter_tokens(): lax.psum_scatter(partial.astype(low).reshape(seqs, -1, partial.shape[-1])...  144 us
    dot_general x24, matrix products, dot(): lax.dot_general(left, right, (((left_dim,), (right_dim,)), ((), ())), pre...  140 us
    all_gather x2, waiting for transfers between devices, gather_tokens(): lax.all_gather(block.reshape(seqs, span, -1), 'shard', axis=1, tiled=True)  131 us
    all_gather x2, waiting for transfers between devices, body(): lax.all_gather(of_replica(w_proj[layer], 0, hidden_own), 'shard', axis=0,...  105 us
    reduce_scatter x4, waiting for transfers between devices, scatter_reps(): lax.psum_scatter(partial.astype(low), 'rep', scatter_dimension=0, tiled=T...  88.8 us
    all_to_all x6, waiting for transfers between devices, swap(): lax.all_to_all(blocks, 'shard', split_axis=0, concat_axis=0, tiled=True)  81.4 us
    all_gather x2, waiting for transfers between devices, body(): lax.all_gather(fc_part.reshape(rows, count * hidden_own), 'shard', axis=0...  71.1 us
  transfers between devices with their start and end apart: 38, of which 30 were waited for; matrix products, arithmetic and copies ran while one was open for 27% of the time, Pallas kernels for 0%

profile of v2, /device:TPU:0, one launch (start us, length us, event | category | flops | bytes accessed | tf_op | source)
XLA Modules:
  0.0 1807.1 jit_solution(5389530944680197468)
XLA Ops:
  14.1 23.3 %all_to_all.45 = bf16[8,136,144]{2,1,0:T(8,128)(2,1)} all-to-all(bf16[8,136,144]{2,1,0:T(8,128)(2,1)S(1)} %copy.171), channel_id=1, replica_groups=mesh['rep'=4,'shard'=8] {'shard'}, dimensions={0} | all-to-all | bytes 626688 | tf_op jit(solution)/shard_map/all_to_all | solution.py:69
  37.7 30.7 %all_gather.75 = f32[8,18,136]{2,1,0:T(8,128)S(1)} all-gather(f32[1,18,136]{2,1,0:T(8,128)S(1)} %all_gather_reshape.3), channel_id=1, replica_groups=mesh['rep'=4,'shard'=8] {'shard'}, dimensions={0}, use_global_device_ids=true | all-gather | bytes 88128 | tf_op jit(solution)/shard_map/all_gather | solution.py:163
  90.1 57.3 %all-gather.33.cloned.1.call-done = bf16[1,2048,1088]{1,2,0:T(8,128)(2,1)} async-done(((bf16[1,256,1088]{1,2,0:T(8,128)(2,1)}), bf16[1,2048,1088]{1,2,0:T(8,128)(2,1)}) %all-gather.33.cloned.1.call-update) | async-done | bytes 4456464 | tf_op jit(solution)/shard_map/all_gather | solution.py:41
  227.4 35.0 %all-gather.37.cloned.1.call-done = bf16[1088,1088]{1,0:T(8,128)(2,1)} async-done(((bf16[136,1088]{1,0:T(8,128)(2,1)}), bf16[1088,1088]{1,0:T(8,128)(2,1)}) %all-gather.37.cloned.1.call-update) | async-done | bytes 2367504 | tf_op jit(solution)/shard_map/all_gather | solution.py:179
  262.4 24.2 %all-gather.35.cloned.1.call-done = bf16[1024,1088]{0,1:T(8,128)(2,1)} async-done(((bf16[256,1088]{0,1:T(8,128)(2,1)}), bf16[1024,1088]{0,1:T(8,128)(2,1)}) %all-gather.35.cloned.1.call-update) | async-done | bytes 2228240 | tf_op jit(solution)/shard_map/all_gather | solution.py:46
  294.1 48.6 %all-gather.49.cloned.1.call-done = bf16[1,1088,1088]{2,1,0:T(8,128)(2,1)} async-done(((bf16[1,136,1088]{2,1,0:T(8,128)(2,1)}), bf16[1,1088,1088]{2,1,0:T(8,128)(2,1)}) %all-gather.49.cloned.1.call-update) | async-done | bytes 2367504 | tf_op jit(solution)/shard_map/all_gather | solution.py:182
  413.6 73.7 %all-gather.51.cloned.1.call-done = bf16[2048,1088]{0,1:T(8,128)(2,1)} async-done(((bf16[256,1088]{0,1:T(8,128)(2,1)}), bf16[2048,1088]{0,1:T(8,128)(2,1)}) %all-gather.51.cloned.1.call-update) | async-done | bytes 4456464 | tf_op jit(solution)/shard_map/all_gather | solution.py:41
  565.8 36.1 %all-gather.41.cloned.1.call-done = bf16[1088,1088]{1,0:T(8,128)(2,1)} async-done(((bf16[136,1088]{1,0:T(8,128)(2,1)}), bf16[1088,1088]{1,0:T(8,128)(2,1)}) %all-gather.41.cloned.1.call-update) | async-done | bytes 2367504 | tf_op jit(solution)/shard_map/all_gather | solution.py:179
  602.0 24.2 %all-gather.39.cloned.1.call-done = bf16[1024,1088]{0,1:T(8,128)(2,1)} async-done(((bf16[256,1088]{0,1:T(8,128)(2,1)}), bf16[1024,1088]{0,1:T(8,128)(2,1)}) %all-gather.39.cloned.1.call-update) | async-done | bytes 2228240 | tf_op jit(solution)/shard_map/all_gather | solution.py:46
  651.5 56.5 %all-gather.57.cloned.1.call-done = bf16[1,1088,1088]{2,1,0:T(8,128)(2,1)} async-done(((bf16[1,136,1088]{2,1,0:T(8,128)(2,1)}), bf16[1,1088,1088]{2,1,0:T(8,128)(2,1)}) %all-gather.57.cloned.1.call-update) | async-done | bytes 2367504 | tf_op jit(solution)/shard_map/all_gather | solution.py:182
  730.8 23.1 %reduce-scatter.31.cloned.1.call-done = bf16[256,1088]{0,1:T(8,128)(2,1)} async-done(((bf16[1024,1088]{0,1:T(8,128)(2,1)}), bf16[256,1088]{0,1:T(8,128)(2,1)}) %reduce-scatter.31.cloned.1.call-update) | async-done | bytes 557072 | tf_op jit(solution)/shard_map/reduce_scatter | solution.py:50
  756.2 32.4 %reduce-scatter.29.cloned.1.call-done = bf16[256,1088]{0,1:T(8,128)(2,1)} async-done(((bf16[1024,1088]{0,1:T(8,128)(2,1)}), bf16[256,1088]{0,1:T(8,128)(2,1)}) %reduce-scatter.29.cloned.1.call-update) | async-done | bytes 557072 | tf_op jit(solution)/shard_map/reduce_scatter | solution.py:50
  799.8 19.9 %all-to-all-done.4 = bf16[8,1,256,192]{2,3,1,0:T(8,128)(2,1)S(1)} async-done(((bf16[8,1,256,192]{2,3,1,0:T(8,128)(2,1)}), bf16[8,1,256,192]{2,3,1,0:T(8,128)(2,1)S(1)}, u32[]{:S(2)}, u32[]{:S(2)}) %all-to-all-start.4) | async-done | bytes 786464 | tf_op jit(solution)/shard_map/all_to_all | solution.py:69
  876.9 90.2 %reduce-scatter.33.cloned.1.call-done = bf16[1,256,1088]{1,2,0:T(8,128)(2,1)} async-done(((bf16[1,2048,1088]{1,2,0:T(8,128)(2,1)}), bf16[1,256,1088]{1,2,0:T(8,128)(2,1)}) %reduce-scatter.33.cloned.1.call-update) | async-done | bytes 557072 | tf_op jit(solution)/shard_map/reduce_scatter | solution.py:59
  1055.3 24.4 %reduce-scatter.35.cloned.1.call-done = bf16[256,1088]{0,1:T(8,128)(2,1)} async-done(((bf16[1024,1088]{0,1:T(8,128)(2,1)}), bf16[256,1088]{0,1:T(8,128)(2,1)}) %reduce-scatter.35.cloned.1.call-update) | async-done | bytes 557072 | tf_op jit(solution)/shard_map/reduce_scatter | solution.py:50
  1092.5 74.8 %reduce-scatter.51.cloned.1.call-done = bf16[136,1088]{1,0:T(8,128)(2,1)} async-done(((bf16[1088,1088]{1,0:T(8,128)(2,1)}), bf16[136,1088]{1,0:T(8,128)(2,1)}) %reduce-scatter.51.cloned.1.call-update) | async-done | bytes 295952
  1169.5 71.0 %reduce-scatter.53.cloned.1.call-done = bf16[136,1088]{1,0:T(8,128)(2,1)} async-done(((bf16[1088,1088]{1,0:T(8,128)(2,1)}), bf16[136,1088]{1,0:T(8,128)(2,1)}) %reduce-scatter.53.cloned.1.call-update) | async-done | bytes 295952
  1356.6 24.4 %reduce-scatter.47.cloned.1.call-done = bf16[136,1088]{1,0:T(8,128)(2,1)} async-done(((bf16[1088,1088]{1,0:T(8,128)(2,1)}), bf16[136,1088]{1,0:T(8,128)(2,1)}) %reduce-scatter.47.cloned.1.call-update) | async-done | bytes 295952
  1382.3 71.6 %reduce-scatter.49.cloned.1.call-done = bf16[136,1088]{1,0:T(8,128)(2,1)} async-done(((bf16[1088,1088]{1,0:T(8,128)(2,1)}), bf16[136,1088]{1,0:T(8,128)(2,1)}) %reduce-scatter.49.cloned.1.call-update) | async-done | bytes 295952
  1457.5 44.4 %reduce-scatter.39.cloned.1.call-done = bf16[1,1088,416]{2,1,0:T(8,128)(2,1)} async-done(((bf16[4,1088,416]{2,1,0:T(8,128)(2,1)}), bf16[1,1088,416]{2,1,0:T(8,128)(2,1)}) %reduce-scatter.39.cloned.1.call-update) | async-done | bytes 905232 | tf_op jit(solution)/shard_map/reduce_scatter | solution.py:278
  1528.1 28.1 %slice_reduce_fusion = (bf16[4,147968]{1,0:T(4,128)(2,1)S(1)}, bf16[4,147968]{1,0:T(4,128)(2,1)}) fusion(bf16[4,2,147968]{2,1,0:T(2,128)(2,1)} %all-gather.67.cloned.1.call-done), kind=kLoop, calls=%fused_computation.151 | loop fusion | bytes 4734976 | tf_op jit(solution)/shard_map/slice | solution.py:285
  1599.2 28.2 %slice_reduce_fusion.1 = (bf16[4,147968]{1,0:T(4,128)(2,1)}, bf16[4,147968]{1,0:T(4,128)(2,1)}) fusion(bf16[4,2,147968]{2,1,0:T(2,128)(2,1)} %all-gather.65.cloned.1.call-done), kind=kLoop, calls=%fused_computation.152 | loop fusion | bytes 4734976 | tf_op jit(solution)/shard_map/slice | solution.py:285
  1661.8 26.1 %all-to-all-done.6 = bf16[8,136,144]{2,1,0:T(8,128)(2,1)} async-done(((bf16[8,136,144]{2,1,0:T(8,128)(2,1)}), bf16[8,136,144]{2,1,0:T(8,128)(2,1)}, u32[]{:S(2)}, u32[]{:S(2)}) %all-to-all-start.6) | async-done | bytes 313376 | tf_op jit(solution)/shard_map/all_to_all | solution.py:69
  1694.0 53.6 %reduce-scatter.37.cloned.1.call-done = bf16[1,256,1088]{1,2,0:T(8,128)(2,1)} async-done(((bf16[1,2048,1088]{1,2,0:T(8,128)(2,1)}), bf16[1,256,1088]{1,2,0:T(8,128)(2,1)}) %reduce-scatter.37.cloned.1.call-update) | async-done | bytes 557072 | tf_op jit(solution)/shard_map/reduce_scatter | solution.py:59
  (796 shorter events, 768.0 us)
Async XLA Ops:
  70.9 133.2 %all-gather.47.cloned.1.call-start = ((), (), s32[]{:S(2)}) async-start(), calls=%async_computation.38 | async-start | bytes 2820096 | tf_op jit(solution)/shard_map/all_gather | solution.py:185
  71.8 190.5 %all-gather.37.cloned.1.call-start = ((), (), s32[]{:S(2)}) async-start(), calls=%async_computation.25 | async-start | bytes 2820096 | tf_op jit(solution)/shard_map/all_gather | solution.py:179
  223.4 119.4 %all-gather.49.cloned.1.call-start = ((), (), s32[]{:S(2)}) async-start(), calls=%async_computation.39 | async-start | bytes 2820096 | tf_op jit(solution)/shard_map/all_gather | solution.py:182
  227.1 154.3 %reduce-scatter.27.cloned.1.call-start = ((), (), s32[]{:S(2)}) async-start(), calls=%async_computation.26 | async-start | bytes 2785280 | tf_op jit(solution)/shard_map/reduce_scatter | solution.py:50
  372.5 114.8 %all-gather.51.cloned.1.call-start = ((), (), s32[]{:S(2)}) async-start(), calls=%async_computation.40 | async-start | bytes 5013504 | tf_op jit(solution)/shard_map/all_gather | solution.py:41
  384.3 158.7 %all-gather.55.cloned.1.call-start = ((), (), s32[]{:S(2)}) async-start(), calls=%async_computation.42 | async-start | bytes 2820096 | tf_op jit(solution)/shard_map/all_gather | solution.py:185
  384.9 217.1 %all-gather.41.cloned.1.call-start = ((), (), s32[]{:S(2)}) async-start(), calls=%async_computation.28 | async-start | bytes 2820096 | tf_op jit(solution)/shard_map/all_gather | solution.py:179
  563.6 144.3 %all-gather.57.cloned.1.call-start = ((), (), s32[]{:S(2)}) async-start(), calls=%async_computation.43 | async-start | bytes 2820096 | tf_op jit(solution)/shard_map/all_gather | solution.py:182
  565.4 188.5 %reduce-scatter.31.cloned.1.call-start = ((), (), s32[]{:S(2)}) async-start(), calls=%async_computation.30 | async-start | bytes 2785280 | tf_op jit(solution)/shard_map/reduce_scatter | solution.py:50
  799.5 167.5 %reduce-scatter.33.cloned.1.call-start = ((), (), s32[]{:S(2)}) async-start(), calls=%async_computation.31 | async-start | bytes 5013504 | tf_op jit(solution)/shard_map/reduce_scatter | solution.py:59
  876.8 119.8 %all-gather.43.cloned.1.call-start = ((), (), s32[]{:S(2)}) async-start(), calls=%async_computation.32 | async-start | bytes 2785280 | tf_op jit(solution)/shard_map/all_gather | solution.py:46
  1011.6 155.7 %reduce-scatter.51.cloned.1.call-start = ((), (), s32[]{:S(2)}) async-start(), calls=%async_computation.53 | async-start | bytes 2820096
  1020.4 220.1 %reduce-scatter.53.cloned.1.call-start = ((), (), s32[]{:S(2)}) async-start(), calls=%async_computation.54 | async-start | bytes 2820096
  1026.5 328.2 %reduce-scatter.45.cloned.1.call-start = ((), (), s32[]{:S(2)}) async-start(), calls=%async_computation.50 | async-start | bytes 940032
  1047.4 333.6 %reduce-scatter.47.cloned.1.call-start = ((), (), s32[]{:S(2)}) async-start(), calls=%async_computation.51 | async-start | bytes 2820096
  1086.3 169.6 %all-to-all-start.5 = ((bf16[8,1,256,192]{2,3,1,0:T(8,128)(2,1)}), bf16[8,1,256,192]{2,3,1,0:T(8,128)(2,1)}, u32[]{:S(2)}, u32[]{:S(2)}) async-start(bf16[8,1,256,192]{2,3,1,0:T(8,128)(2,1)} %bitcast.93), calls=%async_computation.10 | async-start | bytes 1572864 | tf_op jit(solution)/shard_map/all_to_all | solution.py:69
  1091.8 362.1 %reduce-scatter.49.cloned.1.call-start = ((), (), s32[]{:S(2)}) async-start(), calls=%async_computation.52 | async-start | bytes 2820096
  1249.6 252.2 %reduce-scatter.39.cloned.1.call-start = ((), (), s32[]{:S(2)}) async-start(), calls=%async_computation.35 | async-start | bytes 5570560 | tf_op jit(solution)/shard_map/reduce_scatter | solution.py:278
  1332.2 195.9 %all-gather.67.cloned.1.call-start = ((), (), s32[]{:S(2)}) async-start(), calls=%async_computation.48 | async-start | bytes 2959360 | tf_op jit(solution)/shard_map/all_gather | solution.py:284
  1335.5 243.3 %all-gather.63.cloned.1.call-start = ((), (), s32[]{:S(2)}) async-start(), calls=%async_computation.46 | async-start | bytes 2088960 | tf_op jit(solution)/shard_map/all_gather | solution.py:288
  1356.5 242.7 %all-gather.65.cloned.1.call-start = ((), (), s32[]{:S(2)}) async-start(), calls=%async_computation.47 | async-start | bytes 2959360 | tf_op jit(solution)/shard_map/all_gather | solution.py:284
  1457.4 232.2 %reduce-scatter.43.cloned.1.call-start = ((), (), s32[]{:S(2)}) async-start(), calls=%async_computation.49 | async-start | bytes 940032
  1504.4 243.3 %reduce-scatter.37.cloned.1.call-start = ((), (), s32[]{:S(2)}) async-start(), calls=%async_computation.34 | async-start | bytes 5013504 | tf_op jit(solution)/shard_map/reduce_scatter | solution.py:59
  1658.0 120.1 %all-gather.61.cloned.1.call-start = ((), (), s32[]{:S(2)}) async-start(), calls=%async_computation.45 | async-start | bytes 2088960 | tf_op jit(solution)/shard_map/all_gather | solution.py:288
  (201 other events, 4008.6 us)
Sparse Core Ops, SparseCore 0:
  71.0 76.2 all-gather.32
  150.1 53.9 all-gather.46
  206.7 55.6 all-gather.36
  289.2 53.5 all-gather.48
  350.7 30.7 reduce-scatter.26
  409.3 78.0 all-gather.50
  489.6 53.3 all-gather.54
  546.1 55.8 all-gather.40
  654.3 53.5 all-gather.56
  723.1 30.7 reduce-scatter.30
  756.3 32.2 reduce-scatter.28
  876.9 90.0 reduce-scatter.32
  998.6 46.1 reduce-scatter.40
  1047.4 32.2 reduce-scatter.34
  1083.3 83.9 reduce-scatter.50
  1171.5 68.9 reduce-scatter.52
  1243.9 59.8 reduce-scatter.44
  1307.4 73.5 reduce-scatter.46
  1385.2 68.7 reduce-scatter.48
  1456.9 44.9 reduce-scatter.38
  1503.9 24.1 all-gather.66
  1552.2 24.1 all-gather.64
  1580.0 61.1 reduce-scatter.42
  1645.2 102.3 reduce-scatter.36
  (8 shorter events, 175.8 us)
